TPU v7x, 256 devices: a whole 4x4x8 slice. The times are simulated.
256 devices in a mesh: gy: 16 (over z, core), gz: 16 (over x, y).
Axes of the slice: x: 4, y: 4, z: 8, core: 2. Of those that a mesh axis runs over, the one named last changes fastest.
Arguments:
- velocity: float32 [3, 2, 512, 16384], P(None, None, 'gz', 'gy'), may hold values from -6 to 6
- z_lower: float32 [512], P('gz'), may hold values from 2000 to 20500, as said below
- z_upper: float32 [512], P('gz'), may hold values from 2000 to 20500
- z_slope: float32 [512], P('gz'), may hold values from 22 to 72
Outputs:
- projected: float32 [3, 2, 512, 16384], P(None, None, 'gz', 'gy')
Inputs may be any that keep to these rules, and one draw needn't show every extreme that they name: z_lower(k) = 1 / (d(k) c(k)), z_upper(k) = 1 / (d(k+1) c(k)) and z_slope(k) = 1 / (d(k) + d(k+1)) for spacings d(0) to d(512) between neighbouring planes, with c(k) = (d(k) + d(k+1)) / 2.
All inputs are finite; a program needn't handle non-finite values.
Results may differ from a plain program's by a relative error of at most 0.0003.
Values sent between devices are 32-bit elements; how exact they have to be, the bound alone decides.
A program may use at most 128 MiB of HBM per device.

v0:
```python
import math

import jax
import jax.numpy as jnp
from jax import lax
from jax.sharding import PartitionSpec as P

NY = 1024
KX = 16


def with_halo(block, sides, width):
    for axis, dim in sides:
        count = lax.axis_size(axis)
        forward = [(i, i + 1) for i in range(count - 1)]
        backward = [(target, source) for source, target in forward]
        low = lax.ppermute(
            lax.slice_in_dim(block, block.shape[dim] - width, None, axis=dim), axis, forward
        )
        high = lax.ppermute(lax.slice_in_dim(block, 0, width, axis=dim), axis, backward)
        block = jnp.concatenate([low, block, high], axis=dim)
    return block


def prefix_2(part, axis, combine, identity, reverse):
    count = lax.axis_size(axis)
    place = lax.axis_index(axis)
    ahead = count - 1 - place if reverse else place
    gathered = jax.tree.map(lambda a: lax.all_gather(a, axis), part)
    state = jax.tree.map(lambda a, e: jnp.zeros_like(a) + jnp.asarray(e, a.dtype), part, identity)

    def one(hop, state):
        source = count - 1 - hop if reverse else hop
        return combine(
            state, jax.tree.map(lambda a: lax.dynamic_index_in_dim(a, source, 0, False), gathered)
        )

    return lax.fori_loop(0, ahead, one, state)


def fourier_tables(length, orientation):
    positions = jnp.arange(length, dtype=jnp.int32)
    phase_ids = positions[:, None] * positions[None, :] % length
    phases = phase_ids.astype(jnp.float32) * (2.0 * math.pi / length)
    return (jnp.cos(phases), orientation * jnp.sin(phases))


def transform(quantity, orientation, factor):
    cosine, sine_table = fourier_tables(quantity.shape[3], orientation)
    real_part = quantity[:, 0]
    imag_part = quantity[:, 1]

    def product(table, values):
        return jnp.einsum("my,czyk->czmk", table, values, precision=lax.Precision.HIGHEST)

    new_real = product(cosine, real_part) - product(sine_table, imag_part)
    new_imag = product(cosine, imag_part) + product(sine_table, real_part)
    return jnp.stack([new_real, new_imag], axis=1) * factor


def forward_transform(quantity):
    return transform(quantity, -1.0, 1.0)


def to_spectral(quantity):
    return forward_transform(
        lax.all_to_all(quantity, "gy", split_axis=4, concat_axis=3, tiled=True)
    )


def to_physical(quantity):
    return lax.all_to_all(quantity, "gy", split_axis=3, concat_axis=4, tiled=True)


def slope_diff(quantity, slope_coef):
    padded = with_halo(quantity, (("gz", 1),), 1)
    return slope_coef[:, None] * (padded[:, 2:] - padded[:, :-2])


def rotate_by(quantity, wave_value):
    return jnp.stack([-wave_value * quantity[1], wave_value * quantity[0]])


def normalize(matrix):
    return matrix / jnp.max(jnp.abs(matrix), axis=(0, 1), keepdims=True)


def compose(earlier, later):
    return normalize(jnp.einsum("ijl,jkl->ikl", later, earlier, precision=lax.Precision.HIGHEST))


def combine_affine(earlier, later):
    return (
        later[0] + later[2] * earlier[0],
        later[1] + later[2] * earlier[1],
        later[2] * earlier[2],
    )


def solve_lines(coef_below, coef_above, centre, source):
    line_count = centre.shape[1]

    def accumulate(matrix_rows, inputs):
        coef_low, coef_high, middle, driven_real, driven_imag = inputs
        stacked = jnp.stack(
            [
                coef_high * matrix_rows[1],
                middle * matrix_rows[1] - coef_low * matrix_rows[0],
                driven_real * matrix_rows[1] - coef_low * matrix_rows[2],
                driven_imag * matrix_rows[1] - coef_low * matrix_rows[3],
            ]
        )
        return (normalize(stacked), None)

    identity = jnp.broadcast_to(jnp.eye(4, dtype=jnp.float32)[:, :, None], (4, 4, line_count))
    local_map, _ = lax.scan(
        accumulate, identity, (coef_below, coef_above, centre, source[0], source[1])
    )
    prefix = prefix_2(local_map, "gz", compose, identity, False)
    entering = prefix[:, 1, :]

    def forward(state_now, inputs):
        ratio, shift_real, shift_imag = state_now
        coef_low, coef_high, middle, driven_real, driven_imag = inputs
        pivot = middle - coef_low * ratio
        ratio_new = coef_high / pivot
        real_new = (driven_real - coef_low * shift_real) / pivot
        imag_new = (driven_imag - coef_low * shift_imag) / pivot
        return ((ratio_new, real_new, imag_new), (ratio_new, real_new, imag_new))

    initial = (entering[0] / entering[1], entering[2] / entering[1], entering[3] / entering[1])
    _, (ratios, shifts_real, shifts_imag) = lax.scan(
        forward, initial, (coef_below, coef_above, centre, source[0], source[1])
    )

    def backward(state_now, inputs):
        offset_real, offset_imag, weight = state_now
        ratio, shift_real, shift_imag = inputs
        updated = (
            shift_real - ratio * offset_real,
            shift_imag - ratio * offset_imag,
            -ratio * weight,
        )
        return (updated, updated)

    empty = jnp.zeros((line_count,), jnp.float32)
    start_map = (empty, empty, jnp.ones((line_count,), jnp.float32))
    first_map, (offsets_real, offsets_imag, weights) = lax.scan(
        backward, start_map, (ratios, shifts_real, shifts_imag), reverse=True
    )
    following = prefix_2(first_map, "gz", combine_affine, start_map, True)
    pressure_real = offsets_real + weights * following[0][None, :]
    pressure_imag = offsets_imag + weights * following[1][None, :]
    return jnp.stack([pressure_real, pressure_imag])


def shards(velocity, z_lower, z_upper, z_slope):
    blocks = lax.axis_size("gy")
    planes = velocity.shape[2]
    columns = velocity.shape[3]
    y_rows = columns // KX
    wave_local = KX // blocks
    line_count = NY * wave_local
    line_ids = jnp.arange(line_count, dtype=jnp.int32)
    mode_ids = line_ids // wave_local
    wave_y = jnp.where(mode_ids < NY // 2, mode_ids, mode_ids - NY).astype(jnp.float32)
    wave_x = (lax.axis_index("gy") * wave_local + line_ids % wave_local + 1).astype(jnp.float32)
    centre = -(z_lower + z_upper)[:, None] - (wave_x * wave_x + wave_y * wave_y)[None, :]
    shaped = velocity.reshape(3, 2, planes, y_rows, KX)
    spectrum = to_spectral(shaped).reshape(3, 2, planes, line_count)
    divergence = (
        rotate_by(spectrum[0], wave_x)
        + rotate_by(spectrum[1], wave_y)
        + slope_diff(spectrum[2], z_slope)
    )
    pressure = solve_lines(z_lower, z_upper, centre, divergence)
    updated = jnp.stack(
        [
            spectrum[0] - rotate_by(pressure, wave_x),
            spectrum[1] - rotate_by(pressure, wave_y),
            spectrum[2] - slope_diff(pressure, z_slope),
        ]
    )
    restored = transform(updated.reshape(3, 2, planes, NY, wave_local), 1.0, 1.0 / NY)
    return to_physical(restored).reshape(3, 2, planes, columns)


def solution(mesh):
    placed = (P(None, None, "gz", "gy"), P("gz"), P("gz"), P("gz"))
    return jax.shard_map(
        shards, mesh=mesh, in_specs=placed, out_specs=P(None, None, "gz", "gy"), check_vma=False
    )
```

profile of v0, /device:TPU:1, one launch (start us, length us, event | category | flops | bytes accessed | tf_op | source)
XLA Modules:
  0.0 943.9 jit_solution(9092836482615178964)
XLA Ops:
  6.5 2.0 copy.22
  8.5 2.1 copy.23
  10.6 3.1 reshape.298
  13.7 10.0 %all-to-all-start = ((f32[16,1,12288]{2,1,0:T(1,128)}), f32[16,1,12288]{2,1,0:T(1,128)S(1)}, u32[]{:S(2)}, u32[]{:S(2)}) async-start(f32[16,1,12288]{2,1,0:T(1,128)} %reshape.298), calls=%async_computation | async-start | bytes 1572864 | tf_op jit(solution)/shard_map/all_to_all | solution.py:67
  23.9 22.4 %all-to-all-done = f32[16,1,12288]{2,1,0:T(1,128)S(1)} async-done(((f32[16,1,12288]{2,1,0:T(1,128)}), f32[16,1,12288]{2,1,0:T(1,128)S(1)}, u32[]{:S(2)}, u32[]{:S(2)}) %all-to-all-start) | async-done | bytes 786464 | tf_op jit(solution)/shard_map/all_to_all | solution.py:67
  46.8 2.4 reduce.7
  51.5 19.8 %fusion.11 = f32[1024,3,32]{0,2,1:T(8,128)S(1)} fusion(f32[3,2,32,1024,1]{3,2,0,4,1:T(8,128)S(1)} %all_to_all.27), kind=kOutput, calls=%fused_computation.45 | convolution fusion | flops 1223688192 | bytes 786432 | tf_op jit(solution)/shard_map/my,czyk->czmk/dot_general | solution.py:54
  71.3 19.5 %fusion.13 = f32[1024,3,32]{0,2,1:T(8,128)S(1)} fusion(f32[3,2,32,1024,1]{3,2,0,4,1:T(8,128)S(1)} %all_to_all.27), kind=kOutput, calls=%fused_computation.47 | convolution fusion | flops 1223688192 | bytes 786432 | tf_op jit(solution)/shard_map/my,czyk->czmk/dot_general | solution.py:54
  90.8 19.6 %fusion.43 = f32[1024,3,32]{0,2,1:T(8,128)S(1)} fusion(f32[1024,3,32]{0,2,1:T(8,128)S(1)} %fusion.11, f32[3,2,32,1024,1]{3,2,0,4,1:T(8,128)S(1)} %all_to_all.27), kind=kOutput, calls=%fused_computation.67 | convolution fusion | flops 1222737920 | bytes 1179648 | tf_op jit(solution)/shard_map/my,czyk->czmk/dot_general | solution.py:54
  110.4 20.2 %fusion.40 = f32[1024,3,32]{0,2,1:T(8,128)S(1)} fusion(f32[1024,3,32]{0,2,1:T(8,128)S(1)} %fusion.13, f32[3,2,32,1024,1]{3,2,0,4,1:T(8,128)} %copy-done.1), kind=kOutput, calls=%fused_computation.66 | convolution fusion | flops 1222737920 | bytes 1179648 | tf_op jit(solution)/shard_map/my,czyk->czmk/dot_general | solution.py:54
  132.0 4.0 collective-permute-start.1
  137.0 79.4 %while.81 = (s32[]{:T(128)}, f32[4,4,1024]{2,1,0:T(4,128)S(1)}, f32[32]{0:T(128)S(1)}, f32[32,1024]{1,0:T(8,128)S(1)}, f32[32]{0:T(128)S(1)}, /*index=5*/f32[32,1024]{1,0:T(8,128)S(1)}, f32[32,1024]{1,0:T(8,128)S(1)}, s32[]{:T(128)}) while((s32[]{:T(128)}, f32[4,4,1024]{2,1,0:T(4,128)S(1)}, f32[32]{0:T(128)S(1)}, f32[32,1024]{1,0:T(8,128)S(1)}, ...), condition=%wide.region_2.3_spmd, body=%wide.region_0.2_spmd.sunk | while | flops 187394 | bytes 372861 | solution.py:116
  217.1 47.3 %all-gather.6.cloned.1.call-done = f32[64,4,1024]{2,1,0:T(4,128)} async-done(((f32[4,4,1024]{2,1,0:T(4,128)}), f32[64,4,1024]{2,1,0:T(4,128)}) %all-gather.6.cloned.1.call-update) | async-done | bytes 1048592 | tf_op jit(solution)/shard_map/all_gather | solution.py:29
  265.9 6.4 while.82
  272.4 28.4 %fusion.60 = (f32[1024]{0:T(1024)S(1)}, f32[1024]{0:T(1024)S(1)}, f32[1024]{0:T(1024)S(1)}) fusion(f32[4,4,1024]{1,0,2:T(4,128)} %get-tuple-element.446), kind=kLoop, calls=%fused_computation.83 | loop fusion | flops 3072 | bytes 28672 | tf_op jit(solution)/shard_map/div | solution.py:131
  300.9 113.2 %while.83 = (s32[]{:T(128)}, f32[1024]{0:T(1024)S(1)}, f32[1024]{0:T(1024)S(1)}, f32[1024]{0:T(1024)S(1)}, f32[32,1024]{1,0:T(8,128)S(1)}, /*index=5*/f32[32,102...) while((s32[]{:T(128)}, f32[1024]{0:T(1024)S(1)}, ...), condition=%wide.region_7.8_spmd, body=%wide.region_6.7_spmd.sunk | while | flops 9218 | bytes 86201 | solution.py:132
  414.2 13.9 %while.85 = (s32[]{:T(128)}, f32[1024]{0:T(1024)S(1)}, f32[1024]{0:T(1024)S(1)}, f32[1024]{0:T(1024)S(1)}, f32[32,1024]{1,0:T(8,128)S(1)}, /*index=5*/f32[32,102...) while((s32[]{:T(128)}, f32[1024]{0:T(1024)S(1)}, ...), condition=%wide.region_9.10_spmd.clone, body=%wide.region_8.9_spmd.clone.sunk | while | flops 9220 | bytes 86183 | solution.py:148
  428.1 318.7 %all-gather.1 = f32[16384]{0:T(1024)S(1)} all-gather(f32[1024]{0:T(1024)S(1)} %get-tuple-element.452), channel_id=3, replica_groups=mesh['gy'=16,'gz'=16] {'gz'}, dimensions={0}, use_global_device_ids=true | all-gather | bytes 69632 | tf_op jit(solution)/shard_map/all_gather | solution.py:29
  746.8 18.2 %all-gather.2 = f32[16384]{0:T(1024)S(1)} all-gather(f32[1024]{0:T(1024)S(1)} %get-tuple-element.453), channel_id=4, replica_groups=mesh['gy'=16,'gz'=16] {'gz'}, dimensions={0}, use_global_device_ids=true | all-gather | bytes 69632 | tf_op jit(solution)/shard_map/all_gather | solution.py:29
  765.1 15.7 %all-gather.3 = f32[16384]{0:T(1024)S(1)} all-gather(f32[1024]{0:T(1024)S(1)} %get-tuple-element.454), channel_id=5, replica_groups=mesh['gy'=16,'gz'=16] {'gz'}, dimensions={0}, use_global_device_ids=true | all-gather | bytes 69632 | tf_op jit(solution)/shard_map/all_gather | solution.py:29
  783.5 4.2 collective-permute-start.3
  788.4 19.2 %fusion.9 = f32[3,32,1024]{2,1,0:T(8,128)S(1)} fusion(f32[3,2,32,1024,1]{3,2,1,0,4:T(8,128)S(1)} %maximum_bitcast_fusion), kind=kOutput, calls=%fused_computation.43 | convolution fusion | flops 1222639616 | bytes 786432 | tf_op jit(solution)/shard_map/my,czyk->czmk/dot_general | solution.py:54
  807.6 19.2 %fusion.7 = f32[3,32,1024]{2,1,0:T(8,128)S(1)} fusion(f32[3,2,32,1024,1]{3,2,1,0,4:T(8,128)S(1)} %maximum_bitcast_fusion), kind=kOutput, calls=%fused_computation.41 | convolution fusion | flops 1222639616 | bytes 786432 | tf_op jit(solution)/shard_map/my,czyk->czmk/dot_general | solution.py:54
  826.9 19.2 %fusion.49 = f32[3,1,32,1024,1]{3,2,0,4,1:T(8,128)S(1)} fusion(f32[3,32,1024]{2,1,0:T(8,128)S(1)} %fusion.9, f32[3,2,32,1024,1]{3,2,1,0,4:T(8,128)S(1)} %maximum_bitcast_fusion), kind=kOutput, calls=%fused_computation.69 | convolution fusion | flops 1222737920 | bytes 1179648 | tf_op jit(solution)/shard_map/my,czyk->czmk/dot_general | solution.py:54
  846.1 19.2 %fusion.55 = f32[3,1,32,1024,1]{3,2,0,4,1:T(8,128)S(1)} fusion(f32[3,32,1024]{2,1,0:T(8,128)S(1)} %fusion.7, f32[3,2,32,1024,1]{3,2,1,0,4:T(8,128)S(1)} %maximum_bitcast_fusion), kind=kOutput, calls=%fused_computation.71 | convolution fusion | flops 1222737920 | bytes 1179648 | tf_op jit(solution)/shard_map/my,czyk->czmk/dot_general | solution.py:54
  866.2 4.2 copy.27
  870.4 3.9 reshape.300
  874.2 48.5 %all_to_all.33 = f32[16,1,12288]{2,1,0:T(1,128)S(1)} all-to-all(f32[16,1,12288]{2,1,0:T(1,128)} %reshape.300), channel_id=1, replica_groups=mesh['gy'=16,'gz'=16] {'gy'}, dimensions={0} | all-to-all | bytes 1572864 | tf_op jit(solution)/shard_map/all_to_all | solution.py:72
  922.8 3.5 reduce.8
  926.3 3.8 reshape.301
  930.1 3.5 copy.28
  933.5 3.1 copy.29
  (780 shorter events, 213.1 us)
Async XLA Ops:
  10.6 13.2 %copy-start.5 = (f32[32]{0:T(128)S(1)}, f32[32]{0:T(128)}, u32[]{:S(2)}) copy-start(f32[32]{0:T(128)} %param.16) | copy-start | bytes 388
  10.6 13.2 %copy-start.6 = (f32[32]{0:T(128)S(1)}, f32[32]{0:T(128)}, u32[]{:S(2)}) copy-start(f32[32]{0:T(128)} %param.15) | copy-start | bytes 388
  13.7 32.6 %all-to-all-start = ((f32[16,1,12288]{2,1,0:T(1,128)}), f32[16,1,12288]{2,1,0:T(1,128)S(1)}, u32[]{:S(2)}, u32[]{:S(2)}) async-start(f32[16,1,12288]{2,1,0:T(1,128)} %reshape.298), calls=%async_computation | async-start | bytes 1572864 | tf_op jit(solution)/shard_map/all_to_all | solution.py:67
  23.7 240.6 %all-gather.6.cloned.1.call-start = ((), (), s32[]{:S(2)}) async-start(), calls=%async_computation.2 | async-start | bytes 1114112 | tf_op jit(solution)/shard_map/all_gather | solution.py:29
  51.5 39.3 %copy-start.1 = (f32[3,2,32,1024,1]{3,2,0,4,1:T(8,128)}, f32[3,2,32,1024,1]{3,2,0,4,1:T(8,128)S(1)}, u32[]{:S(2)}) copy-start(f32[3,2,32,1024,1]{3,2,0,4,1:T(8,128)S(1)} %all_to_all.27) | copy-start | bytes 2359300
  110.4 26.4 %copy-start.4 = (f32[32]{0:T(128)S(1)}, f32[32]{0:T(128)}, u32[]{:S(2)}) copy-start(f32[32]{0:T(128)} %param.17) | copy-start | bytes 388
  130.7 5.4 collective-permute-start
  132.0 4.8 collective-permute-start.1
  216.4 0.6 copy-start
  216.4 0.7 copy-start.2
  216.4 49.6 %copy-start.3 = (f32[32,1024]{1,0:T(8,128)}, f32[32,1024]{1,0:T(8,128)S(1)}, u32[]{:S(2)}) copy-start(f32[32,1024]{1,0:T(8,128)S(1)} %get-tuple-element.1112) | copy-start | bytes 393220
  782.2 5.6 collective-permute-start.2
  783.5 4.8 collective-permute-start.3
Sparse Core Ops, SparseCore 0:
  217.1 47.1 all-gather.5
where the time goes:
time: 963 us; the launch traced here: 944 us
  blocking collectives  401 us (42%)
  matrix products  156 us (16%)
  local copies, waits for them, and re-layouts  153 us (16%)
  other arithmetic  115 us (12%)
  waiting for transfers between devices  70.9 us (7%)
  starting transfers between devices  20.8 us (2%)
  between operations  14.3 us (1%)
  loops' own time  12.9 us (1%)
    all_gather x3, blocking collectives, prefix_2(): gathered = jax.tree.map(lambda a: lax.all_gather(a, axis), part)  353 us
    dot_general x8, matrix products, product(): jnp.einsum('my,czyk->czmk', table, values, precision=lax.Precision.HIGHEST)  156 us
    dynamic_slice x320, local copies, waits for them, and re-layouts, solve_lines(): lax.scan(accumulate, identity, (coef_below, coef_above, centre, source[0]...  101 us
    all_to_all x1, blocking collectives, to_physical(): lax.all_to_all(quantity, 'gy', split_axis=3, concat_axis=4, tiled=True)  48.5 us
    all_gather x1, waiting for transfers between devices, prefix_2(): gathered = jax.tree.map(lambda a: lax.all_gather(a, axis), part)  47.3 us
    mul x32, other arithmetic, accumulate(): coef_high * matrix_rows[1]  38.6 us
    div x32, other arithmetic, forward(): imag_new = (driven_imag - coef_low * shift_imag) / pivot  37.9 us
    div x1, other arithmetic, solve_lines(): entering[3] / entering[1]  28.4 us
  transfers between devices with their start and end apart: 6, of which 4 were waited for; matrix products, arithmetic and copies ran while one was open for 0% of the time, Pallas kernels for 0%

commit v1 on v0

v1 whole, which is shorter than its diff:
```python
import functools

import jax
import jax.numpy as jnp
import ml_dtypes
import numpy as np
from jax import lax
from jax.experimental import pallas as pl
from jax.experimental.pallas import tpu as pltpu
from jax.sharding import PartitionSpec as P

NY = 1024
KX = 16
LANES = 128
MESH = pl.DeviceIdType.MESH


def fourier_tables():
    place = np.arange(256)
    y = 64 * ((place % 128) // 32) + 32 * (place // 128) + place % 32

    def pair(m):
        phase = 2.0 * np.pi * ((y[:, None] * m[None, :]) % NY) / NY
        return np.cos(phase), np.sin(phase)

    c0, s0 = pair(4 * np.arange(128))
    s0[:, 0] = (-1.0) ** y
    c2, s2 = pair(4 * np.arange(128) + 2)
    c1, s1 = pair(4 * np.arange(256) + 1)
    table = np.concatenate([c0, s0, c2, s2, c1, s1], axis=1)

    def split(values):
        high = values.astype(ml_dtypes.bfloat16)
        low = (values - high.astype(np.float64)).astype(ml_dtypes.bfloat16)
        return np.stack([high, low])

    return split(table), split(table.T / NY)


def dot(a, b):
    return jnp.dot(a, b, preferred_element_type=jnp.float32)


def product(values, high, low):
    top = values.astype(jnp.bfloat16)
    rest = (values - top.astype(jnp.float32)).astype(jnp.bfloat16)
    rows = values.shape[0]
    both = dot(jnp.concatenate([top, rest], axis=0), high)
    return both[:rows] + both[rows:] + dot(top, low)


def kernel(
    planes, gy, gz,
    vel, zl, zu, zs, ftab_hbm, itab_hbm, out,
    ftab, itab, rows_buf, send_f, recv_f, send_b, recv_b,
    halo_send, halo_recv, vhat, field_re, field_im,
    inv_piv, mult, ratio, beta, gamma,
    mat_all, rhs_all, red_den, red_bden, red_psi, red_b31, red_br, red_r, red_e, red_phi, red_f,
    grad,
    tab_sem, halo_ssem, halo_rsem, f_ssem, f_rsem, b_ssem, b_rsem, m_ssem, m_rsem, r_ssem, r_rsem,
):
    me = lax.axis_index("gy")
    mz = lax.axis_index("gz")
    f32 = jnp.float32

    barrier = pltpu.get_barrier_semaphore()

    def greet(o, _):
        pl.semaphore_signal(barrier, inc=1, device_id={"gy": lax.rem(me + o, gy)}, device_id_type=MESH)
        pl.semaphore_signal(barrier, inc=1, device_id={"gz": lax.rem(mz + o, gz)}, device_id_type=MESH)
        return 0

    lax.fori_loop(1, gy, greet, 0)
    copy_ft = pltpu.make_async_copy(ftab_hbm, ftab, tab_sem.at[0])
    copy_it = pltpu.make_async_copy(itab_hbm, itab, tab_sem.at[1])
    copy_ft.start()
    copy_it.start()

    def stage(f, re, im):
        for c in range(4):
            a = slice(c * 128, c * 128 + 128)
            b = slice(512 + c * 128, 512 + c * 128 + 128)
            block = jnp.concatenate([re[:, a], im[:, a], re[:, b], im[:, b]], axis=0)
            rows_buf[c * 128:(c + 1) * 128, :] = block.T
        for j in range(KX):
            send_f[f, j] = rows_buf[pl.ds(j, 32, stride=16), :]

    def y_copy(src, dst, ssem, rsem, f, o, slot_src, slot_dst):
        return pltpu.make_async_remote_copy(
            src_ref=src.at[f, slot_src], dst_ref=dst.at[f, slot_dst],
            send_sem=ssem.at[f, o], recv_sem=rsem.at[f, o],
            device_id={"gy": lax.rem(me + o, gy)}, device_id_type=MESH)

    def y_send(src, dst, ssem, rsem, f):
        def one(o, _):
            y_copy(src, dst, ssem, rsem, f, o, lax.rem(me + o, gy), me).start()
            return 0

        lax.fori_loop(1, gy, one, 0)
        dst[f, me] = src[f, me]

    def y_wait_recv(src, dst, ssem, rsem, f):
        def one(o, _):
            d = lax.rem(me + gy - o, gy)
            y_copy(src, dst, ssem, rsem, f, o, d, d).wait_recv()
            return 0

        lax.fori_loop(1, gy, one, 0)

    def y_wait_send(src, dst, ssem, rsem, f):
        def one(o, _):
            y_copy(src, dst, ssem, rsem, f, o, lax.rem(me + o, gy), me).wait_send()
            return 0

        lax.fori_loop(1, gy, one, 0)

    def z_copy(buf, ssem, rsem, o, slot):
        return pltpu.make_async_remote_copy(
            src_ref=buf.at[slot], dst_ref=buf.at[slot],
            send_sem=ssem.at[o], recv_sem=rsem.at[o],
            device_id={"gz": lax.rem(mz + o, gz)}, device_id_type=MESH)

    def z_send(buf, ssem, rsem):
        def one(o, _):
            z_copy(buf, ssem, rsem, o, mz).start()
            return 0

        lax.fori_loop(1, gz, one, 0)

    def z_wait_recv(buf, ssem, rsem):
        def one(o, _):
            z_copy(buf, ssem, rsem, o, lax.rem(mz + gz - o, gz)).wait_recv()
            return 0

        lax.fori_loop(1, gz, one, 0)

    def z_wait_send(buf, ssem, rsem):
        def one(o, _):
            z_copy(buf, ssem, rsem, o, mz).wait_send()
            return 0

        lax.fori_loop(1, gz, one, 0)

    def halo_copies(f):
        up = pltpu.make_async_remote_copy(
            src_ref=halo_send.at[f, 0], dst_ref=halo_recv.at[f, 0],
            send_sem=halo_ssem.at[f, 0], recv_sem=halo_rsem.at[f, 0],
            device_id={"gz": lax.rem(mz + 1, gz)}, device_id_type=MESH)
        down = pltpu.make_async_remote_copy(
            src_ref=halo_send.at[f, 1], dst_ref=halo_recv.at[f, 1],
            send_sem=halo_ssem.at[f, 1], recv_sem=halo_rsem.at[f, 1],
            device_id={"gz": lax.rem(mz + gz - 1, gz)}, device_id_type=MESH)
        return up, down

    plane_id = lax.broadcasted_iota(jnp.int32, (planes, LANES), 0)

    def column(ref):
        def one(k, col):
            return jnp.where(plane_id == k, ref[k], col)

        return lax.fori_loop(0, planes, one, jnp.zeros((planes, LANES), f32))

    slope = column(zs)
    slope_wide = jnp.concatenate([slope] * 8, axis=1)
    kx_lane = (lax.broadcasted_iota(jnp.int32, (1, NY), 1) % KX + 1).astype(f32)

    def slope_diff(values, f, part):
        low = jnp.where(mz > 0, halo_recv[f, 0, part:part + 1, :], 0.0)
        high = jnp.where(mz < gz - 1, halo_recv[f, 1, part:part + 1, :], 0.0)
        above = jnp.concatenate([values[1:], high], axis=0)
        below = jnp.concatenate([low, values[:-1]], axis=0)
        return slope_wide * (above - below)

    for part in range(2):
        halo_send[0, 0, part:part + 1, :] = vel[2, part, planes - 1:planes, :]
        halo_send[0, 1, part:part + 1, :] = vel[2, part, 0:1, :]
    stage(1, vel[1, 0], vel[1, 1])
    pl.semaphore_wait(barrier, 2 * (gy - 1))
    halo_w = halo_copies(0)
    halo_w[0].start()
    halo_w[1].start()
    y_send(send_f, recv_f, f_ssem, f_rsem, 1)

    halo_w[0].wait_recv()
    halo_w[1].wait_recv()
    stage(0, slope_diff(vel[2, 0], 0, 0) - kx_lane * vel[0, 1], slope_diff(vel[2, 1], 0, 1) + kx_lane * vel[0, 0])
    y_send(send_f, recv_f, f_ssem, f_rsem, 0)

    row = lax.broadcasted_iota(jnp.int32, (8, LANES), 0)
    lane = lax.broadcasted_iota(jnp.int32, (8, LANES), 1)
    offset = jnp.where(row < 2, 0, jnp.where(row < 4, 2, jnp.where((row == 4) | (row == 6), 1, -511)))
    ky_int = 4 * lane + offset
    ky_int = jnp.where((row == 1) | (row == 3) | (row >= 6), -ky_int, ky_int)
    ky_int = jnp.where((row == 1) & (lane == 0), -512, ky_int)
    ky = ky_int.astype(f32)
    kx = (me + 1).astype(f32)
    square = kx * kx + ky * ky

    def rows_of(k):
        return pl.ds(pl.multiple_of(k * 8, 8), 8)

    def factor(k, state):
        r, g = state
        low, up = zl[k], zu[k]
        inverse = 1.0 / (-(low + up) - square - low * r)
        m = low * inverse
        r = up * inverse
        g = -m * g
        inv_piv[rows_of(k), :] = inverse
        mult[rows_of(k), :] = m
        ratio[rows_of(k), :] = r
        beta[rows_of(k), :] = g
        return r, g

    zero = jnp.zeros((8, LANES), f32)
    one_v = jnp.ones((8, LANES), f32)
    lax.fori_loop(0, planes, factor, (zero, one_v))

    def unfold(i, state):
        b, g = state
        k = planes - 1 - i
        r = ratio[rows_of(k), :]
        b = beta[rows_of(k), :] - r * b
        g = -r * g
        beta[rows_of(k), :] = b
        gamma[rows_of(k), :] = g
        return b, g

    b0, g0 = lax.fori_loop(0, planes, unfold, (zero, one_v))
    last = slice((planes - 1) * 8, planes * 8)
    mat_all[mz, 0] = b0
    mat_all[mz, 1] = g0
    mat_all[mz, 2] = beta[last, :]
    mat_all[mz, 3] = gamma[last, :]
    z_send(mat_all, m_ssem, m_rsem)
    z_wait_recv(mat_all, m_ssem, m_rsem)

    red_r[0] = zero
    red_e[0, 0] = zero
    red_e[0, 1] = zero

    def reduce_matrix(d, r):
        den = 1.0 / (1.0 - mat_all[d, 0] * r)
        psi = mat_all[d, 1] * den
        br = mat_all[d, 2] * r
        red_den[d] = den
        red_bden[d] = mat_all[d, 0] * den
        red_psi[d] = psi
        red_br[d] = br
        r = mat_all[d, 3] + br * psi
        red_r[d + 1] = r
        return r

    lax.fori_loop(0, gz, reduce_matrix, zero)

    copy_ft.wait()
    first_lane = lax.broadcasted_iota(jnp.int32, (planes, LANES), 1) == 0

    def forward(f):
        quarters = []
        for q in range(4):
            block = recv_f[f, 4 * q:4 * q + 4].reshape(LANES, LANES).T
            quarters.append(jnp.concatenate([block[:64], block[64:]], axis=1))
        a = quarters[0] + quarters[2]
        b = quarters[0] - quarters[2]
        c = quarters[1] + quarters[3]
        e = quarters[1] - quarters[3]
        turned = jnp.concatenate([e[planes:], -e[:planes]], axis=0)
        spectra = []
        for first, z in ((0, a + c), (256, a - c)):
            both = product(z, ftab[0, :, first:first + 256], ftab[1, :, first:first + 256])
            rc, rs = both[:planes, :128], both[:planes, 128:]
            ic, is_ = both[planes:, :128], both[planes:, 128:]
            if first == 0:
                rs0, is0 = jnp.where(first_lane, 0.0, rs), jnp.where(first_lane, 0.0, is_)
                spectra.append((rc + is0, ic - rs0))
                spectra.append((jnp.where(first_lane, rs, rc - is_), jnp.where(first_lane, is_, ic + rs)))
            else:
                spectra.append((rc + is_, ic - rs))
                spectra.append((rc - is_, ic + rs))
        both = product(jnp.concatenate([b + turned, b - turned], axis=0), ftab[0, :, 512:], ftab[1, :, 512:])
        for half in range(2):
            cos, sin = both[:, half * 128:half * 128 + 128], both[:, 256 + half * 128:384 + half * 128]
            spectra.append((cos[:planes] + sin[planes:2 * planes], cos[planes:2 * planes] - sin[:planes]))
        for half in range(2):
            cos, sin = both[:, half * 128:half * 128 + 128], both[:, 256 + half * 128:384 + half * 128]
            spectra.append((cos[2 * planes:3 * planes] - sin[3 * planes:], cos[3 * planes:] + sin[2 * planes:3 * planes]))
        return spectra

    y_wait_recv(send_f, recv_f, f_ssem, f_rsem, 1)
    for s, (re, im) in enumerate(forward(1)):
        ky_row = ky[s:s + 1, :]
        vhat[s, 0] = -ky_row * im
        vhat[s, 1] = ky_row * re
    y_wait_recv(send_f, recv_f, f_ssem, f_rsem, 0)
    for s, (re, im) in enumerate(forward(0)):
        field_re[pl.ds(s, planes, stride=8), :] = re + vhat[s, 0]
        field_im[pl.ds(s, planes, stride=8), :] = im + vhat[s, 1]

    def down(k, state):
        sr, si = state
        inverse, m = inv_piv[rows_of(k), :], mult[rows_of(k), :]
        sr = field_re[rows_of(k), :] * inverse - m * sr
        si = field_im[rows_of(k), :] * inverse - m * si
        field_re[rows_of(k), :] = sr
        field_im[rows_of(k), :] = si
        return sr, si

    lax.fori_loop(0, planes, down, (zero, zero), unroll=True)

    def back(i, state):
        ar, ai = state
        k = planes - 1 - i
        r = ratio[rows_of(k), :]
        ar = field_re[rows_of(k), :] - r * ar
        ai = field_im[rows_of(k), :] - r * ai
        field_re[rows_of(k), :] = ar
        field_im[rows_of(k), :] = ai
        return ar, ai

    ar, ai = lax.fori_loop(0, planes, back, (zero, zero), unroll=True)
    rhs_all[mz, 0] = ar
    rhs_all[mz, 1] = ai
    rhs_all[mz, 2] = field_re[last, :]
    rhs_all[mz, 3] = field_im[last, :]
    z_send(rhs_all, r_ssem, r_rsem)
    z_wait_recv(rhs_all, r_ssem, r_rsem)

    def reduce_rhs(d, state):
        er, ei = state
        den, bden, br, b31 = red_den[d], red_bden[d], red_br[d], mat_all[d, 2]
        pr = den * rhs_all[d, 0] + bden * er
        pi = den * rhs_all[d, 1] + bden * ei
        er = rhs_all[d, 2] + b31 * er + br * pr
        ei = rhs_all[d, 3] + b31 * ei + br * pi
        red_phi[d, 0] = pr
        red_phi[d, 1] = pi
        red_e[d + 1, 0] = er
        red_e[d + 1, 1] = ei
        return er, ei

    lax.fori_loop(0, gz, reduce_rhs, (zero, zero), unroll=True)
    red_f[gz, 0] = zero
    red_f[gz, 1] = zero

    def reduce_back(i, state):
        fr, fi = state
        d = gz - 1 - i
        psi = red_psi[d]
        fr = red_phi[d, 0] + psi * fr
        fi = red_phi[d, 1] + psi * fi
        red_f[d, 0] = fr
        red_f[d, 1] = fi
        return fr, fi

    lax.fori_loop(0, gz, reduce_back, (zero, zero), unroll=True)
    before = [red_e[mz, part] + red_r[mz] * red_f[mz, part] for part in range(2)]
    after = [red_f[mz + 1, part] for part in range(2)]

    def finish(k, _):
        b, g = beta[rows_of(k), :], gamma[rows_of(k), :]
        field_re[rows_of(k), :] = field_re[rows_of(k), :] + b * before[0] + g * after[0]
        field_im[rows_of(k), :] = field_im[rows_of(k), :] + b * before[1] + g * after[1]
        return 0

    lax.fori_loop(0, planes, finish, 0, unroll=True)

    copy_it.wait()

    def inverse(f, spectra):
        parts = []
        for first in (0, 256):
            (pr, pi), (nr, ni) = spectra[first // 128], spectra[first // 128 + 1]
            cr, sr, ci, si = pr + nr, ni - pi, pi + ni, pr - nr
            if first == 0:
                cr, sr = jnp.where(first_lane, pr, cr), jnp.where(first_lane, nr, sr)
                ci, si = jnp.where(first_lane, pi, ci), jnp.where(first_lane, ni, si)
            z = jnp.concatenate([jnp.concatenate([cr, sr], axis=1), jnp.concatenate([ci, si], axis=1)], axis=0)
            parts.append(product(z, itab[0, first:first + 256, :], itab[1, first:first + 256, :]))
        (ar, ai), (br, bi), (cr, ci), (dr, di) = spectra[4:]
        z = jnp.concatenate([
            jnp.concatenate([ar, br, -ai, -bi], axis=1),
            jnp.concatenate([ai, bi, ar, br], axis=1),
            jnp.concatenate([cr, dr, ci, di], axis=1),
            jnp.concatenate([ci, di, -cr, -dr], axis=1)], axis=0)
        odd = product(z, itab[0, 512:, :], itab[1, 512:, :])
        g1, g3 = odd[:64], odd[64:]
        s02, d02 = parts[0] + parts[1], parts[0] - parts[1]
        s13, d13 = g1 + g3, g1 - g3
        turned = jnp.concatenate([-d13[planes:], d13[:planes]], axis=0)
        for q, value in enumerate((s02 + s13, d02 + turned, s02 - s13, d02 - turned)):
            block = jnp.concatenate([value[:, :128], value[:, 128:]], axis=0).T
            send_b[f, 4 * q:4 * q + 4] = block.reshape(4, 32, LANES)

    tiles = [(field_re[pl.ds(s, planes, stride=8), :], field_im[pl.ds(s, planes, stride=8), :]) for s in range(8)]
    inverse(0, tiles)
    y_send(send_b, recv_b, b_ssem, b_rsem, 0)
    inverse(1, [(-ky[s:s + 1, :] * im, ky[s:s + 1, :] * re) for s, (re, im) in enumerate(tiles)])
    y_send(send_b, recv_b, b_ssem, b_rsem, 1)

    def unstage(f):
        for j in range(KX):
            rows_buf[pl.ds(j, 32, stride=16), :] = recv_b[f, j]
        for c in range(4):
            block = rows_buf[c * 128:(c + 1) * 128, :].T
            for h in range(2):
                for part in range(2):
                    first = h * 64 + part * 32
                    grad[part, :, h * 512 + c * 128:h * 512 + c * 128 + 128] = block[first:first + 32]

    y_wait_recv(send_b, recv_b, b_ssem, b_rsem, 0)
    unstage(0)
    for part in range(2):
        halo_send[1, 0, part:part + 1, :] = grad[part, planes - 1:planes, :]
        halo_send[1, 1, part:part + 1, :] = grad[part, 0:1, :]
    halo_p = halo_copies(1)
    halo_p[0].start()
    halo_p[1].start()
    out[0, 0] = vel[0, 0] + kx_lane * grad[1]
    out[0, 1] = vel[0, 1] - kx_lane * grad[0]
    halo_p[0].wait_recv()
    halo_p[1].wait_recv()
    for part in range(2):
        out[2, part] = vel[2, part] - slope_diff(grad[part], 1, part)
    y_wait_recv(send_b, recv_b, b_ssem, b_rsem, 1)
    unstage(1)
    for part in range(2):
        out[1, part] = vel[1, part] - grad[part]

    for copy in (*halo_w, *halo_p):
        copy.wait_send()
    for f in range(2):
        y_wait_send(send_f, recv_f, f_ssem, f_rsem, f)
        y_wait_send(send_b, recv_b, b_ssem, b_rsem, f)
    z_wait_send(mat_all, m_ssem, m_rsem)
    z_wait_send(rhs_all, r_ssem, r_rsem)


def shards(velocity, z_lower, z_upper, z_slope):
    gy, gz = lax.axis_size("gy"), lax.axis_size("gz")
    planes = velocity.shape[2]
    ftab, itab = (jnp.asarray(table) for table in fourier_tables())
    f32 = jnp.float32
    vmem = pl.BlockSpec(memory_space=pltpu.VMEM)
    smem = pl.BlockSpec(memory_space=pltpu.SMEM)
    hbm = pl.BlockSpec(memory_space=pl.ANY)
    lines = (planes * 8, LANES)
    dma = pltpu.SemaphoreType.DMA
    return pl.pallas_call(
        functools.partial(kernel, planes, gy, gz),
        out_shape=jax.ShapeDtypeStruct(velocity.shape, f32),
        in_specs=[vmem, smem, smem, smem, hbm, hbm],
        out_specs=vmem,
        scratch_shapes=[
            pltpu.VMEM(ftab.shape, jnp.bfloat16),
            pltpu.VMEM(itab.shape, jnp.bfloat16),
            pltpu.VMEM((512, LANES), f32),
            pltpu.VMEM((2, gy, 32, LANES), f32),
            pltpu.VMEM((2, gy, 32, LANES), f32),
            pltpu.VMEM((2, gy, 32, LANES), f32),
            pltpu.VMEM((2, gy, 32, LANES), f32),
            pltpu.VMEM((2, 2, 2, NY), f32),
            pltpu.VMEM((2, 2, 2, NY), f32),
            pltpu.VMEM((8, 2, planes, LANES), f32),
            pltpu.VMEM(lines, f32),
            pltpu.VMEM(lines, f32),
            pltpu.VMEM(lines, f32),
            pltpu.VMEM(lines, f32),
            pltpu.VMEM(lines, f32),
            pltpu.VMEM(lines, f32),
            pltpu.VMEM(lines, f32),
            pltpu.VMEM((gz, 4, 8, LANES), f32),
            pltpu.VMEM((gz, 4, 8, LANES), f32),
            pltpu.VMEM((gz, 8, LANES), f32),
            pltpu.VMEM((gz, 8, LANES), f32),
            pltpu.VMEM((gz, 8, LANES), f32),
            pltpu.VMEM((gz, 8, LANES), f32),
            pltpu.VMEM((gz, 8, LANES), f32),
            pltpu.VMEM((gz + 1, 8, LANES), f32),
            pltpu.VMEM((gz + 1, 2, 8, LANES), f32),
            pltpu.VMEM((gz, 2, 8, LANES), f32),
            pltpu.VMEM((gz + 1, 2, 8, LANES), f32),
            pltpu.VMEM((2, planes, NY), f32),
            dma((2,)), dma((2, 2)), dma((2, 2)),
            dma((2, gy)), dma((2, gy)), dma((2, gy)), dma((2, gy)),
            dma((gz,)), dma((gz,)), dma((gz,)), dma((gz,)),
        ],
        compiler_params=pltpu.CompilerParams(
            collective_id=0, has_side_effects=True, vmem_limit_bytes=40 * 1024 * 1024
        ),
        name="project",
    )(velocity, z_lower, z_upper, z_slope, ftab, itab)


def solution(mesh):
    placed = (P(None, None, "gz", "gy"), P("gz"), P("gz"), P("gz"))
    return jax.shard_map(
        shards, mesh=mesh, in_specs=placed, out_specs=P(None, None, "gz", "gy"), check_vma=False
    )
```

time: 963 us -> 56.1 us (0.06); the launches traced: 944 us -> 55.9 us
  blocking collectives: 401 us -> 0 us
  matrix products: 156 us -> 0 us
  local copies, waits for them, and re-layouts: 153 us -> 6.43 us
  other arithmetic: 115 us -> 0 us
  waiting for transfers between devices: 70.9 us -> 0 us
  Pallas kernels: 0 us -> 49.5 us
  starting transfers between devices: 20.8 us -> 0 us
  between operations: 14.3 us -> 0.02 us
  loops' own time: 12.9 us -> 0 us
    all_gather x3 -> x0, blocking collectives: 353 us -> none  [prefix_2(): gathered = jax.tree.map(lambda a: lax.all_gather(a, axis), part)]
    dot_general x8 -> x0, matrix products: 156 us -> none  [product(): jnp.einsum('my,czyk->czmk', table, values, precision=lax.Precision.HIGHEST)]
    dynamic_slice x350 -> x0, local copies, waits for them, and re-layouts: 102 us -> none  [the longest x320 101 us: solve_lines(): lax.scan(accumulate, identity, (coef_below, coef_above, centre, source[0]...]
    div x65 -> x0, other arithmetic: 67 us -> none  [the longest x32 37.9 us: forward(): imag_new = (driven_imag - coef_low * shift_imag) / pivot]
    pallas_call x0 -> x1, Pallas kernels: none -> 49.5 us  [shards(): pl.pallas_call(functools.partial(kernel, planes, gy, gz), out_shape=jax.S...]
    all_to_all x1 -> x0, blocking collectives: 48.5 us -> none  [to_physical(): lax.all_to_all(quantity, 'gy', split_axis=3, concat_axis=4, tiled=True)]
    all_gather x1 -> x0, waiting for transfers between devices: 47.3 us -> none  [prefix_2(): gathered = jax.tree.map(lambda a: lax.all_gather(a, axis), part)]
    mul x66 -> x0, other arithmetic: 39.9 us -> none  [the longest x32 38.6 us: accumulate(): coef_high * matrix_rows[1]]
  transfers between devices with their start and end apart: 6 -> 0, of which waited for: 4 -> 0; matrix products, arithmetic and copies ran while one was open for 0% -> 0% of each run, Pallas kernels for 0% -> 0%
where the time goes in v1:
time: 56.1 us; the launch traced here: 55.9 us
  Pallas kernels  49.5 us (88%)
  local copies, waits for them, and re-layouts  6.43 us (11%)
    pallas_call x1, Pallas kernels, shards(): pl.pallas_call(functools.partial(kernel, planes, gy, gz), out_shape=jax.S...  49.5 us
    unnamed x13, local copies, waits for them, and re-layouts  6.43 us

profile of v1, /device:TPU:1, one launch (start us, length us, event | category | flops | bytes accessed | tf_op | source)
XLA Modules:
  0.0 55.9 jit_solution(18364652560108524489)
XLA Ops:
  0.0 0.0 copy-start
  0.0 1.2 %copy-done = bf16[2,1024,256]{2,1,0:T(8,128)(2,1)S(1)} copy-done((bf16[2,1024,256]{2,1,0:T(8,128)(2,1)S(1)}, bf16[2,1024,256]{2,1,0:T(8,128)(2,1)}, u32[]{:S(2)}) %copy-start) | copy-done | bytes 1048600
  1.2 0.0 copy-start.1
  1.2 1.2 %copy-done.1 = bf16[2,256,1024]{2,1,0:T(8,128)(2,1)S(1)} copy-done((bf16[2,256,1024]{2,1,0:T(8,128)(2,1)S(1)}, bf16[2,256,1024]{2,1,0:T(8,128)(2,1)}, u32[]{:S(2)}) %copy-start.1) | copy-done | bytes 1048600
  2.5 0.0 copy-start.2
  2.5 1.1 %copy-done.2 = f32[3,2,32,1024]{3,2,1,0:T(8,128)S(1)} copy-done((f32[3,2,32,1024]{3,2,1,0:T(8,128)S(1)}, f32[3,2,32,1024]{3,2,1,0:T(8,128)}, u32[]{:S(2)}) %copy-start.2) | copy-done | bytes 786456
  3.6 0.0 copy-start.3
  3.6 0.7 %copy-done.3 = f32[32]{0:T(128)S(1)} copy-done((f32[32]{0:T(128)S(1)}, f32[32]{0:T(128)}, u32[]{:S(2)}) %copy-start.3) | copy-done | bytes 152
  4.2 0.0 copy-start.4
  4.2 0.7 %copy-done.4 = f32[32]{0:T(128)S(1)} copy-done((f32[32]{0:T(128)S(1)}, f32[32]{0:T(128)}, u32[]{:S(2)}) %copy-start.4) | copy-done | bytes 152
  4.9 0.0 copy-start.5
  4.9 0.7 %copy-done.5 = f32[32]{0:T(128)S(1)} copy-done((f32[32]{0:T(128)S(1)}, f32[32]{0:T(128)}, u32[]{:S(2)}) %copy-start.5) | copy-done | bytes 152
  5.6 49.5 %project.1 = f32[3,2,32,1024]{3,2,1,0:T(8,128)S(1)} custom-call(f32[3,2,32,1024]{3,2,1,0:T(8,128)S(1)} %copy-done.2, f32[32]{0:T(128)S(1)} %copy-done.3, f32[32]{0:T(128)S(1)} %copy-done.4, f32[32]{0:T(128)S(1)} %copy-done.5, bf16[2,256,1024]{2,1,0:T(8,128)(2,1)S(1)} %copy-done.1, bf16[2,1024,256]{2,1,0:T(8,128)(2,1)S(1)} %copy-done), custom_call_target="tpu_custom_call" | custom-call | tf_op jit(solution)/shard_map/project/pallas_call | solution.py:449
  55.0 0.9 %copy.8 = f32[3,2,32,1024]{3,2,1,0:T(8,128)} copy(f32[3,2,32,1024]{3,2,1,0:T(8,128)S(1)} %project.1) | data formatting | bytes 1572864
Async XLA Ops:
  0.0 1.2 %copy-start = (bf16[2,1024,256]{2,1,0:T(8,128)(2,1)S(1)}, bf16[2,1024,256]{2,1,0:T(8,128)(2,1)}, u32[]{:S(2)}) copy-start(bf16[2,1024,256]{2,1,0:T(8,128)(2,1)} %constant.5.clone.itab_hbm) | copy-start | bytes 3145732
  1.2 1.2 %copy-start.1 = (bf16[2,256,1024]{2,1,0:T(8,128)(2,1)S(1)}, bf16[2,256,1024]{2,1,0:T(8,128)(2,1)}, u32[]{:S(2)}) copy-start(bf16[2,256,1024]{2,1,0:T(8,128)(2,1)} %constant.4.clone.ftab_hbm) | copy-start | bytes 3145732
  2.5 1.1 %copy-start.2 = (f32[3,2,32,1024]{3,2,1,0:T(8,128)S(1)}, f32[3,2,32,1024]{3,2,1,0:T(8,128)}, u32[]{:S(2)}) copy-start(f32[3,2,32,1024]{3,2,1,0:T(8,128)} %vel.1) | copy-start | bytes 2359300
  3.6 0.7 %copy-start.3 = (f32[32]{0:T(128)S(1)}, f32[32]{0:T(128)}, u32[]{:S(2)}) copy-start(f32[32]{0:T(128)} %zl.1) | copy-start | bytes 388
  4.2 0.7 %copy-start.4 = (f32[32]{0:T(128)S(1)}, f32[32]{0:T(128)}, u32[]{:S(2)}) copy-start(f32[32]{0:T(128)} %zu.1) | copy-start | bytes 388
  4.9 0.7 %copy-start.5 = (f32[32]{0:T(128)S(1)}, f32[32]{0:T(128)}, u32[]{:S(2)}) copy-start(f32[32]{0:T(128)} %zs.1) | copy-start | bytes 388

commit v2 on v1

--- a/solution.py
+++ b/solution.py
@@ -51,18 +51,28 @@
 
 def kernel(
     planes, gy, gz,
-    vel, zl, zu, zs, ftab_hbm, itab_hbm, out,
-    ftab, itab, rows_buf, send_f, recv_f, send_b, recv_b,
+    vel_hbm, zl_hbm, zu_hbm, zs_hbm, ftab_hbm, itab_hbm, out_hbm,
+    vel, out, zl, zu, zs, ftab, itab, rows_buf, send_f, recv_f, send_b, recv_b,
     halo_send, halo_recv, vhat, field_re, field_im,
     inv_piv, mult, ratio, beta, gamma,
     mat_all, rhs_all, red_den, red_bden, red_psi, red_b31, red_br, red_r, red_e, red_phi, red_f,
     grad,
-    tab_sem, halo_ssem, halo_rsem, f_ssem, f_rsem, b_ssem, b_rsem, m_ssem, m_rsem, r_ssem, r_rsem,
+    in_sem, out_sem, halo_ssem, halo_rsem, f_ssem, f_rsem, b_ssem, b_rsem, m_ssem, m_rsem, r_ssem, r_rsem,
 ):
     me = lax.axis_index("gy")
     mz = lax.axis_index("gz")
     f32 = jnp.float32
 
+    copy_in = [pltpu.make_async_copy(vel_hbm.at[c], vel.at[c], in_sem.at[c]) for c in range(3)]
+    copy_z = [
+        pltpu.make_async_copy(src, dst, in_sem.at[3 + i])
+        for i, (src, dst) in enumerate(((zl_hbm, zl), (zu_hbm, zu), (zs_hbm, zs)))
+    ]
+    copy_ft = pltpu.make_async_copy(ftab_hbm, ftab, in_sem.at[6])
+    copy_it = pltpu.make_async_copy(itab_hbm, itab, in_sem.at[7])
+    copy_out = [pltpu.make_async_copy(out.at[c], out_hbm.at[c], out_sem.at[c]) for c in range(3)]
+    copy_in[1].start()
+    copy_in[2].start()
     barrier = pltpu.get_barrier_semaphore()
 
     def greet(o, _):
@@ -71,10 +81,8 @@
         return 0
 
     lax.fori_loop(1, gy, greet, 0)
-    copy_ft = pltpu.make_async_copy(ftab_hbm, ftab, tab_sem.at[0])
-    copy_it = pltpu.make_async_copy(itab_hbm, itab, tab_sem.at[1])
-    copy_ft.start()
-    copy_it.start()
+    for copy in (copy_z[2], copy_in[0], copy_z[0], copy_z[1], copy_ft, copy_it):
+        copy.start()
 
     def stage(f, re, im):
         for c in range(4):
@@ -160,32 +168,38 @@
 
         return lax.fori_loop(0, planes, one, jnp.zeros((planes, LANES), f32))
 
-    slope = column(zs)
-    slope_wide = jnp.concatenate([slope] * 8, axis=1)
     kx_lane = (lax.broadcasted_iota(jnp.int32, (1, NY), 1) % KX + 1).astype(f32)
 
-    def slope_diff(values, f, part):
+    def slope_diff(values, f, part, slope_wide):
         low = jnp.where(mz > 0, halo_recv[f, 0, part:part + 1, :], 0.0)
         high = jnp.where(mz < gz - 1, halo_recv[f, 1, part:part + 1, :], 0.0)
         above = jnp.concatenate([values[1:], high], axis=0)
         below = jnp.concatenate([low, values[:-1]], axis=0)
         return slope_wide * (above - below)
 
+    copy_in[1].wait()
+    stage(1, vel[1, 0], vel[1, 1])
+    copy_in[2].wait()
     for part in range(2):
         halo_send[0, 0, part:part + 1, :] = vel[2, part, planes - 1:planes, :]
         halo_send[0, 1, part:part + 1, :] = vel[2, part, 0:1, :]
-    stage(1, vel[1, 0], vel[1, 1])
     pl.semaphore_wait(barrier, 2 * (gy - 1))
     halo_w = halo_copies(0)
     halo_w[0].start()
     halo_w[1].start()
     y_send(send_f, recv_f, f_ssem, f_rsem, 1)
 
+    copy_z[2].wait()
+    slope = column(zs)
+    slope_wide = jnp.concatenate([slope] * 8, axis=1)
+    copy_in[0].wait()
     halo_w[0].wait_recv()
     halo_w[1].wait_recv()
-    stage(0, slope_diff(vel[2, 0], 0, 0) - kx_lane * vel[0, 1], slope_diff(vel[2, 1], 0, 1) + kx_lane * vel[0, 0])
+    stage(0, slope_diff(vel[2, 0], 0, 0, slope_wide) - kx_lane * vel[0, 1], slope_diff(vel[2, 1], 0, 1, slope_wide) + kx_lane * vel[0, 0])
     y_send(send_f, recv_f, f_ssem, f_rsem, 0)
 
+    copy_z[0].wait()
+    copy_z[1].wait()
     row = lax.broadcasted_iota(jnp.int32, (8, LANES), 0)
     lane = lax.broadcasted_iota(jnp.int32, (8, LANES), 1)
     offset = jnp.where(row < 2, 0, jnp.where(row < 4, 2, jnp.where((row == 4) | (row == 6), 1, -511)))
@@ -418,14 +432,17 @@
     halo_p[1].start()
     out[0, 0] = vel[0, 0] + kx_lane * grad[1]
     out[0, 1] = vel[0, 1] - kx_lane * grad[0]
+    copy_out[0].start()
     halo_p[0].wait_recv()
     halo_p[1].wait_recv()
     for part in range(2):
-        out[2, part] = vel[2, part] - slope_diff(grad[part], 1, part)
+        out[2, part] = vel[2, part] - slope_diff(grad[part], 1, part, slope_wide)
+    copy_out[2].start()
     y_wait_recv(send_b, recv_b, b_ssem, b_rsem, 1)
     unstage(1)
     for part in range(2):
         out[1, part] = vel[1, part] - grad[part]
+    copy_out[1].start()
 
     for copy in (*halo_w, *halo_p):
         copy.wait_send()
@@ -434,6 +451,8 @@
         y_wait_send(send_b, recv_b, b_ssem, b_rsem, f)
     z_wait_send(mat_all, m_ssem, m_rsem)
     z_wait_send(rhs_all, r_ssem, r_rsem)
+    for copy in copy_out:
+        copy.wait()
 
 
 def shards(velocity, z_lower, z_upper, z_slope):
@@ -441,17 +460,20 @@
     planes = velocity.shape[2]
     ftab, itab = (jnp.asarray(table) for table in fourier_tables())
     f32 = jnp.float32
-    vmem = pl.BlockSpec(memory_space=pltpu.VMEM)
-    smem = pl.BlockSpec(memory_space=pltpu.SMEM)
     hbm = pl.BlockSpec(memory_space=pl.ANY)
     lines = (planes * 8, LANES)
     dma = pltpu.SemaphoreType.DMA
     return pl.pallas_call(
         functools.partial(kernel, planes, gy, gz),
         out_shape=jax.ShapeDtypeStruct(velocity.shape, f32),
-        in_specs=[vmem, smem, smem, smem, hbm, hbm],
-        out_specs=vmem,
+        in_specs=[pl.BlockSpec(memory_space=pltpu.HBM)] * 6,
+        out_specs=hbm,
         scratch_shapes=[
+            pltpu.VMEM(velocity.shape, f32),
+            pltpu.VMEM(velocity.shape, f32),
+            pltpu.SMEM((planes,), f32),
+            pltpu.SMEM((planes,), f32),
+            pltpu.SMEM((planes,), f32),
             pltpu.VMEM(ftab.shape, jnp.bfloat16),
             pltpu.VMEM(itab.shape, jnp.bfloat16),
             pltpu.VMEM((512, LANES), f32),
@@ -481,7 +503,7 @@
             pltpu.VMEM((gz, 2, 8, LANES), f32),
             pltpu.VMEM((gz + 1, 2, 8, LANES), f32),
             pltpu.VMEM((2, planes, NY), f32),
-            dma((2,)), dma((2, 2)), dma((2, 2)),
+            dma((8,)), dma((3,)), dma((2, 2)), dma((2, 2)),
             dma((2, gy)), dma((2, gy)), dma((2, gy)), dma((2, gy)),
             dma((gz,)), dma((gz,)), dma((gz,)), dma((gz,)),
         ],
@@ -489,7 +511,7 @@
             collective_id=0, has_side_effects=True, vmem_limit_bytes=40 * 1024 * 1024
         ),
         name="project",
-    )(velocity, z_lower, z_upper, z_slope, ftab, itab)
+    )(*(pltpu.with_memory_space_constraint(a, pltpu.HBM) for a in (velocity, z_lower, z_upper, z_slope, ftab, itab)))
 
 
 def solution(mesh):

time: 56.1 us -> 49.9 us (0.89)
  local copies, waits for them, and re-layouts: 6.43 us -> 0.88 us
    unnamed x13 -> x1, local copies, waits for them, and re-layouts: 6.43 us -> 0.88 us
where the time goes in v2:
time: 49.9 us; the launch traced here: 49.8 us
  Pallas kernels  49 us (98%)
  local copies, waits for them, and re-layouts  0.88 us (2%)
    pallas_call x1, Pallas kernels, shards(): pl.pallas_call(functools.partial(kernel, planes, gy, gz), out_shape=jax.S...  49 us

profile of v2, /device:TPU:1, one launch (start us, length us, event | category | flops | bytes accessed | tf_op | source)
XLA Modules:
  0.0 49.8 jit_solution(11802148311919904586)
XLA Ops:
  0.0 49.0 %project.1 = f32[3,2,32,1024]{3,2,1,0:T(8,128)S(1)} custom-call(f32[3,2,32,1024]{3,2,1,0:T(8,128)} %vel_hbm.1, f32[32]{0:T(128)} %zl_hbm.1, f32[32]{0:T(128)} %zu_hbm.1, f32[32]{0:T(128)} %zs_hbm.1, bf16[2,256,1024]{2,1,0:T(8,128)(2,1)} %constant.4.clone.ftab_hbm, bf16[2,1024,256]{2,1,0:T(8,128)(2,1)} %constant.5.clone.itab_hbm), custom_call_target="tpu_custom_call" | custom-call | tf_op jit(solution)/shard_map/project/pallas_call | solution.py:466
  49.0 0.9 %copy.8 = f32[3,2,32,1024]{3,2,1,0:T(8,128)} copy(f32[3,2,32,1024]{3,2,1,0:T(8,128)S(1)} %project.1) | data formatting | bytes 1572864

commit v3 on v2

--- a/solution.py
+++ b/solution.py
@@ -13,6 +13,11 @@
 KX = 16
 LANES = 128
 MESH = pl.DeviceIdType.MESH
+Y_ORDER = [(dz, c) for dz in (4, 3, -3, 2, -2, 1, -1) for c in (0, 1)] + [(0, 1)]
+Z_ORDER = sorted(
+    ((dx, dy) for dx in (2, 1, -1, 0) for dy in (2, 1, -1, 0) if (dx, dy) != (0, 0)),
+    key=lambda pair: -abs(pair[0]) - abs(pair[1]),
+)
 
 
 def fourier_tables():
@@ -75,12 +80,19 @@
     copy_in[2].start()
     barrier = pltpu.get_barrier_semaphore()
 
-    def greet(o, _):
-        pl.semaphore_signal(barrier, inc=1, device_id={"gy": lax.rem(me + o, gy)}, device_id_type=MESH)
-        pl.semaphore_signal(barrier, inc=1, device_id={"gz": lax.rem(mz + o, gz)}, device_id_type=MESH)
-        return 0
-
-    lax.fori_loop(1, gy, greet, 0)
+    def y_partner(o, sign):
+        dz, c = Y_ORDER[o]
+        return lax.rem(me // 2 + sign * dz + gy // 2, gy // 2) * 2 + lax.rem(me + c, 2)
+
+    def z_partner(o, sign):
+        dx, dy = Z_ORDER[o]
+        return lax.rem(mz // 4 + sign * dx + 4, 4) * 4 + lax.rem(mz + sign * dy + 4, 4)
+
+    y_all, z_all = range(len(Y_ORDER)), range(len(Z_ORDER))
+    for o in y_all:
+        pl.semaphore_signal(barrier, inc=1, device_id={"gy": y_partner(o, 1)}, device_id_type=MESH)
+    for o in z_all:
+        pl.semaphore_signal(barrier, inc=1, device_id={"gz": z_partner(o, 1)}, device_id_type=MESH)
     for copy in (copy_z[2], copy_in[0], copy_z[0], copy_z[1], copy_ft, copy_it):
         copy.start()
 
@@ -97,57 +109,39 @@
         return pltpu.make_async_remote_copy(
             src_ref=src.at[f, slot_src], dst_ref=dst.at[f, slot_dst],
             send_sem=ssem.at[f, o], recv_sem=rsem.at[f, o],
-            device_id={"gy": lax.rem(me + o, gy)}, device_id_type=MESH)
+            device_id={"gy": y_partner(o, 1)}, device_id_type=MESH)
 
     def y_send(src, dst, ssem, rsem, f):
-        def one(o, _):
-            y_copy(src, dst, ssem, rsem, f, o, lax.rem(me + o, gy), me).start()
-            return 0
-
-        lax.fori_loop(1, gy, one, 0)
+        for o in y_all:
+            y_copy(src, dst, ssem, rsem, f, o, y_partner(o, 1), me).start()
         dst[f, me] = src[f, me]
 
     def y_wait_recv(src, dst, ssem, rsem, f):
-        def one(o, _):
-            d = lax.rem(me + gy - o, gy)
+        for o in y_all:
+            d = y_partner(o, -1)
             y_copy(src, dst, ssem, rsem, f, o, d, d).wait_recv()
-            return 0
-
-        lax.fori_loop(1, gy, one, 0)
 
     def y_wait_send(src, dst, ssem, rsem, f):
-        def one(o, _):
-            y_copy(src, dst, ssem, rsem, f, o, lax.rem(me + o, gy), me).wait_send()
-            return 0
-
-        lax.fori_loop(1, gy, one, 0)
+        for o in y_all:
+            y_copy(src, dst, ssem, rsem, f, o, y_partner(o, 1), me).wait_send()
 
     def z_copy(buf, ssem, rsem, o, slot):
         return pltpu.make_async_remote_copy(
             src_ref=buf.at[slot], dst_ref=buf.at[slot],
             send_sem=ssem.at[o], recv_sem=rsem.at[o],
-            device_id={"gz": lax.rem(mz + o, gz)}, device_id_type=MESH)
+            device_id={"gz": z_partner(o, 1)}, device_id_type=MESH)
 
     def z_send(buf, ssem, rsem):
-        def one(o, _):
+        for o in z_all:
             z_copy(buf, ssem, rsem, o, mz).start()
-            return 0
-
-        lax.fori_loop(1, gz, one, 0)
 
     def z_wait_recv(buf, ssem, rsem):
-        def one(o, _):
-            z_copy(buf, ssem, rsem, o, lax.rem(mz + gz - o, gz)).wait_recv()
-            return 0
-
-        lax.fori_loop(1, gz, one, 0)
+        for o in z_all:
+            z_copy(buf, ssem, rsem, o, z_partner(o, -1)).wait_recv()
 
     def z_wait_send(buf, ssem, rsem):
-        def one(o, _):
+        for o in z_all:
             z_copy(buf, ssem, rsem, o, mz).wait_send()
-            return 0
-
-        lax.fori_loop(1, gz, one, 0)
 
     def halo_copies(f):
         up = pltpu.make_async_remote_copy(
@@ -183,7 +177,7 @@
     for part in range(2):
         halo_send[0, 0, part:part + 1, :] = vel[2, part, planes - 1:planes, :]
         halo_send[0, 1, part:part + 1, :] = vel[2, part, 0:1, :]
-    pl.semaphore_wait(barrier, 2 * (gy - 1))
+    pl.semaphore_wait(barrier, len(Y_ORDER) + len(Z_ORDER))
     halo_w = halo_copies(0)
     halo_w[0].start()
     halo_w[1].start()

time: 49.9 us -> 47.4 us (0.950)
  Pallas kernels: 49 us -> 46.4 us
    pallas_call x1, Pallas kernels: 49 us -> 46.4 us  [shards(): pl.pallas_call(functools.partial(kernel, planes, gy, gz), out_shape=jax.S...]
where the time goes in v3:
time: 47.4 us; the launch traced here: 47.3 us
  Pallas kernels  46.4 us (98%)
  local copies, waits for them, and re-layouts  0.88 us (2%)
    pallas_call x1, Pallas kernels, shards(): pl.pallas_call(functools.partial(kernel, planes, gy, gz), out_shape=jax.S...  46.4 us

profile of v3, /device:TPU:1, one launch (start us, length us, event | category | flops | bytes accessed | tf_op | source)
XLA Modules:
  0.0 47.3 jit_solution(16461832655938183290)
XLA Ops:
  0.0 46.4 %project.1 = f32[3,2,32,1024]{3,2,1,0:T(8,128)S(1)} custom-call(f32[3,2,32,1024]{3,2,1,0:T(8,128)} %vel_hbm.1, f32[32]{0:T(128)} %zl_hbm.1, f32[32]{0:T(128)} %zu_hbm.1, f32[32]{0:T(128)} %zs_hbm.1, bf16[2,256,1024]{2,1,0:T(8,128)(2,1)} %constant.4.clone.ftab_hbm, bf16[2,1024,256]{2,1,0:T(8,128)(2,1)} %constant.5.clone.itab_hbm), custom_call_target="tpu_custom_call" | custom-call | tf_op jit(solution)/shard_map/project/pallas_call | solution.py:460
  46.4 0.9 %copy.8 = f32[3,2,32,1024]{3,2,1,0:T(8,128)} copy(f32[3,2,32,1024]{3,2,1,0:T(8,128)S(1)} %project.1) | data formatting | bytes 1572864

commit v4 on v3

--- a/solution.py
+++ b/solution.py
@@ -13,7 +13,7 @@
 KX = 16
 LANES = 128
 MESH = pl.DeviceIdType.MESH
-Y_ORDER = [(dz, c) for dz in (4, 3, -3, 2, -2, 1, -1) for c in (0, 1)] + [(0, 1)]
+Y_ORDER = (4, 3, -3, 2, -2, 1, -1)
 Z_ORDER = sorted(
     ((dx, dy) for dx in (2, 1, -1, 0) for dy in (2, 1, -1, 0) if (dx, dy) != (0, 0)),
     key=lambda pair: -abs(pair[0]) - abs(pair[1]),
@@ -56,13 +56,13 @@
 
 def kernel(
     planes, gy, gz,
-    vel_hbm, zl_hbm, zu_hbm, zs_hbm, ftab_hbm, itab_hbm, out_hbm,
-    vel, out, zl, zu, zs, ftab, itab, rows_buf, send_f, recv_f, send_b, recv_b,
+    vel_hbm, zl_hbm, zu_hbm, zs_hbm, ftab_hbm, itab_hbm, out,
+    vel, zl, zu, zs, ftab, itab, rows_buf, send_f, recv_f, send_b, recv_b,
     halo_send, halo_recv, vhat, field_re, field_im,
     inv_piv, mult, ratio, beta, gamma,
     mat_all, rhs_all, red_den, red_bden, red_psi, red_b31, red_br, red_r, red_e, red_phi, red_f,
-    grad,
-    in_sem, out_sem, halo_ssem, halo_rsem, f_ssem, f_rsem, b_ssem, b_rsem, m_ssem, m_rsem, r_ssem, r_rsem,
+    grad, grad_q,
+    in_sem, halo_ssem, halo_rsem, f_ssem, f_rsem, b_ssem, b_rsem, m_ssem, m_rsem, r_ssem, r_rsem,
 ):
     me = lax.axis_index("gy")
     mz = lax.axis_index("gz")
@@ -75,22 +75,24 @@
     ]
     copy_ft = pltpu.make_async_copy(ftab_hbm, ftab, in_sem.at[6])
     copy_it = pltpu.make_async_copy(itab_hbm, itab, in_sem.at[7])
-    copy_out = [pltpu.make_async_copy(out.at[c], out_hbm.at[c], out_sem.at[c]) for c in range(3)]
     copy_in[1].start()
     copy_in[2].start()
     barrier = pltpu.get_barrier_semaphore()
 
-    def y_partner(o, sign):
-        dz, c = Y_ORDER[o]
-        return lax.rem(me // 2 + sign * dz + gy // 2, gy // 2) * 2 + lax.rem(me + c, 2)
+    chips, chip, core = gy // 2, me // 2, lax.rem(me, 2)
+    mate = me + 1 - 2 * core
+
+    def y_partner(dz, c):
+        return lax.rem(chip + dz + chips, chips) * 2 + c
 
     def z_partner(o, sign):
         dx, dy = Z_ORDER[o]
         return lax.rem(mz // 4 + sign * dx + 4, 4) * 4 + lax.rem(mz + sign * dy + 4, 4)
 
-    y_all, z_all = range(len(Y_ORDER)), range(len(Z_ORDER))
-    for o in y_all:
-        pl.semaphore_signal(barrier, inc=1, device_id={"gy": y_partner(o, 1)}, device_id_type=MESH)
+    z_all = range(len(Z_ORDER))
+    y_all = [y_partner(dz, c) for dz in Y_ORDER for c in range(2)] + [mate]
+    for g in y_all:
+        pl.semaphore_signal(barrier, inc=1, device_id={"gy": g}, device_id_type=MESH)
     for o in z_all:
         pl.semaphore_signal(barrier, inc=1, device_id={"gz": z_partner(o, 1)}, device_id_type=MESH)
     for copy in (copy_z[2], copy_in[0], copy_z[0], copy_z[1], copy_ft, copy_it):
@@ -105,25 +107,26 @@
         for j in range(KX):
             send_f[f, j] = rows_buf[pl.ds(j, 32, stride=16), :]
 
-    def y_copy(src, dst, ssem, rsem, f, o, slot_src, slot_dst):
+    def y_copy(src, dst, ssem, rsem, f, g):
         return pltpu.make_async_remote_copy(
-            src_ref=src.at[f, slot_src], dst_ref=dst.at[f, slot_dst],
-            send_sem=ssem.at[f, o], recv_sem=rsem.at[f, o],
-            device_id={"gy": y_partner(o, 1)}, device_id_type=MESH)
-
-    def y_send(src, dst, ssem, rsem, f):
-        for o in y_all:
-            y_copy(src, dst, ssem, rsem, f, o, y_partner(o, 1), me).start()
-        dst[f, me] = src[f, me]
+            src_ref=src.at[f, g], dst_ref=dst.at[f, me],
+            send_sem=ssem.at[f, g], recv_sem=rsem.at[f, me],
+            device_id={"gy": g}, device_id_type=MESH)
+
+    def y_send(src, dst, ssem, rsem, f, partners):
+        for g in partners:
+            y_copy(src, dst, ssem, rsem, f, g).start()
 
     def y_wait_recv(src, dst, ssem, rsem, f):
-        for o in y_all:
-            d = y_partner(o, -1)
-            y_copy(src, dst, ssem, rsem, f, o, d, d).wait_recv()
+        for g in y_all:
+            pltpu.make_async_remote_copy(
+                src_ref=src.at[f, g], dst_ref=dst.at[f, g],
+                send_sem=ssem.at[f, g], recv_sem=rsem.at[f, g],
+                device_id={"gy": g}, device_id_type=MESH).wait_recv()
 
     def y_wait_send(src, dst, ssem, rsem, f):
-        for o in y_all:
-            y_copy(src, dst, ssem, rsem, f, o, y_partner(o, 1), me).wait_send()
+        for g in y_all:
+            y_copy(src, dst, ssem, rsem, f, g).wait_send()
 
     def z_copy(buf, ssem, rsem, o, slot):
         return pltpu.make_async_remote_copy(
@@ -177,11 +180,13 @@
     for part in range(2):
         halo_send[0, 0, part:part + 1, :] = vel[2, part, planes - 1:planes, :]
         halo_send[0, 1, part:part + 1, :] = vel[2, part, 0:1, :]
-    pl.semaphore_wait(barrier, len(Y_ORDER) + len(Z_ORDER))
+    pl.semaphore_wait(barrier, len(y_all) + len(Z_ORDER))
     halo_w = halo_copies(0)
     halo_w[0].start()
     halo_w[1].start()
-    y_send(send_f, recv_f, f_ssem, f_rsem, 1)
+    to_core = [[y_partner(dz, c) for dz in Y_ORDER] for c in range(2)]
+    y_send(send_f, recv_f, f_ssem, f_rsem, 1, to_core[0] + [mate] + to_core[1][:4])
+    recv_f[1, me] = send_f[1, me]
 
     copy_z[2].wait()
     slope = column(zs)
@@ -190,7 +195,10 @@
     halo_w[0].wait_recv()
     halo_w[1].wait_recv()
     stage(0, slope_diff(vel[2, 0], 0, 0, slope_wide) - kx_lane * vel[0, 1], slope_diff(vel[2, 1], 0, 1, slope_wide) + kx_lane * vel[0, 0])
-    y_send(send_f, recv_f, f_ssem, f_rsem, 0)
+    y_send(send_f, recv_f, f_ssem, f_rsem, 0, to_core[0] + [mate])
+    y_send(send_f, recv_f, f_ssem, f_rsem, 1, to_core[1][4:])
+    y_send(send_f, recv_f, f_ssem, f_rsem, 0, to_core[1])
+    recv_f[0, me] = send_f[0, me]
 
     copy_z[0].wait()
     copy_z[1].wait()
@@ -241,25 +249,6 @@
     mat_all[mz, 2] = beta[last, :]
     mat_all[mz, 3] = gamma[last, :]
     z_send(mat_all, m_ssem, m_rsem)
-    z_wait_recv(mat_all, m_ssem, m_rsem)
-
-    red_r[0] = zero
-    red_e[0, 0] = zero
-    red_e[0, 1] = zero
-
-    def reduce_matrix(d, r):
-        den = 1.0 / (1.0 - mat_all[d, 0] * r)
-        psi = mat_all[d, 1] * den
-        br = mat_all[d, 2] * r
-        red_den[d] = den
-        red_bden[d] = mat_all[d, 0] * den
-        red_psi[d] = psi
-        red_br[d] = br
-        r = mat_all[d, 3] + br * psi
-        red_r[d + 1] = r
-        return r
-
-    lax.fori_loop(0, gz, reduce_matrix, zero)
 
     copy_ft.wait()
     first_lane = lax.broadcasted_iota(jnp.int32, (planes, LANES), 1) == 0
@@ -332,6 +321,25 @@
     rhs_all[mz, 2] = field_re[last, :]
     rhs_all[mz, 3] = field_im[last, :]
     z_send(rhs_all, r_ssem, r_rsem)
+
+    z_wait_recv(mat_all, m_ssem, m_rsem)
+    red_r[0] = zero
+    red_e[0, 0] = zero
+    red_e[0, 1] = zero
+
+    def reduce_matrix(d, r):
+        den = 1.0 / (1.0 - mat_all[d, 0] * r)
+        psi = mat_all[d, 1] * den
+        br = mat_all[d, 2] * r
+        red_den[d] = den
+        red_bden[d] = mat_all[d, 0] * den
+        red_psi[d] = psi
+        red_br[d] = br
+        r = mat_all[d, 3] + br * psi
+        red_r[d + 1] = r
+        return r
+
+    lax.fori_loop(0, gz, reduce_matrix, zero)
     z_wait_recv(rhs_all, r_ssem, r_rsem)
 
     def reduce_rhs(d, state):
@@ -402,11 +410,13 @@
 
     tiles = [(field_re[pl.ds(s, planes, stride=8), :], field_im[pl.ds(s, planes, stride=8), :]) for s in range(8)]
     inverse(0, tiles)
-    y_send(send_b, recv_b, b_ssem, b_rsem, 0)
+    y_send(send_b, recv_b, b_ssem, b_rsem, 0, y_all)
+    recv_b[0, me] = send_b[0, me]
     inverse(1, [(-ky[s:s + 1, :] * im, ky[s:s + 1, :] * re) for s, (re, im) in enumerate(tiles)])
-    y_send(send_b, recv_b, b_ssem, b_rsem, 1)
-
-    def unstage(f):
+    y_send(send_b, recv_b, b_ssem, b_rsem, 1, y_all)
+    recv_b[1, me] = send_b[1, me]
+
+    def unstage(f, grad):
         for j in range(KX):
             rows_buf[pl.ds(j, 32, stride=16), :] = recv_b[f, j]
         for c in range(4):
@@ -416,8 +426,14 @@
                     first = h * 64 + part * 32
                     grad[part, :, h * 512 + c * 128:h * 512 + c * 128 + 128] = block[first:first + 32]
 
+    for copy in halo_w:
+        copy.wait_send()
+    for f in range(2):
+        y_wait_send(send_f, recv_f, f_ssem, f_rsem, f)
+    z_wait_send(mat_all, m_ssem, m_rsem)
+    z_wait_send(rhs_all, r_ssem, r_rsem)
     y_wait_recv(send_b, recv_b, b_ssem, b_rsem, 0)
-    unstage(0)
+    unstage(0, grad)
     for part in range(2):
         halo_send[1, 0, part:part + 1, :] = grad[part, planes - 1:planes, :]
         halo_send[1, 1, part:part + 1, :] = grad[part, 0:1, :]
@@ -426,27 +442,19 @@
     halo_p[1].start()
     out[0, 0] = vel[0, 0] + kx_lane * grad[1]
     out[0, 1] = vel[0, 1] - kx_lane * grad[0]
-    copy_out[0].start()
+    y_wait_send(send_b, recv_b, b_ssem, b_rsem, 0)
+    y_wait_recv(send_b, recv_b, b_ssem, b_rsem, 1)
+    unstage(1, grad_q)
+    for part in range(2):
+        out[1, part] = vel[1, part] - grad_q[part]
     halo_p[0].wait_recv()
     halo_p[1].wait_recv()
     for part in range(2):
         out[2, part] = vel[2, part] - slope_diff(grad[part], 1, part, slope_wide)
-    copy_out[2].start()
-    y_wait_recv(send_b, recv_b, b_ssem, b_rsem, 1)
-    unstage(1)
-    for part in range(2):
-        out[1, part] = vel[1, part] - grad[part]
-    copy_out[1].start()
-
-    for copy in (*halo_w, *halo_p):
+
+    for copy in halo_p:
         copy.wait_send()
-    for f in range(2):
-        y_wait_send(send_f, recv_f, f_ssem, f_rsem, f)
-        y_wait_send(send_b, recv_b, b_ssem, b_rsem, f)
-    z_wait_send(mat_all, m_ssem, m_rsem)
-    z_wait_send(rhs_all, r_ssem, r_rsem)
-    for copy in copy_out:
-        copy.wait()
+    y_wait_send(send_b, recv_b, b_ssem, b_rsem, 1)
 
 
 def shards(velocity, z_lower, z_upper, z_slope):
@@ -461,9 +469,8 @@
         functools.partial(kernel, planes, gy, gz),
         out_shape=jax.ShapeDtypeStruct(velocity.shape, f32),
         in_specs=[pl.BlockSpec(memory_space=pltpu.HBM)] * 6,
-        out_specs=hbm,
+        out_specs=pl.BlockSpec(memory_space=pltpu.VMEM),
         scratch_shapes=[
-            pltpu.VMEM(velocity.shape, f32),
             pltpu.VMEM(velocity.shape, f32),
             pltpu.SMEM((planes,), f32),
             pltpu.SMEM((planes,), f32),
@@ -497,7 +504,8 @@
             pltpu.VMEM((gz, 2, 8, LANES), f32),
             pltpu.VMEM((gz + 1, 2, 8, LANES), f32),
             pltpu.VMEM((2, planes, NY), f32),
-            dma((8,)), dma((3,)), dma((2, 2)), dma((2, 2)),
+            pltpu.VMEM((2, planes, NY), f32),
+            dma((8,)), dma((2, 2)), dma((2, 2)),
             dma((2, gy)), dma((2, gy)), dma((2, gy)), dma((2, gy)),
             dma((gz,)), dma((gz,)), dma((gz,)), dma((gz,)),
         ],

time: 47.4 us -> 45.5 us (0.960)
  Pallas kernels: 46.4 us -> 44.6 us
    pallas_call x1, Pallas kernels: 46.4 us -> 44.6 us  [shards(): pl.pallas_call(functools.partial(kernel, planes, gy, gz), out_shape=jax.S...]
where the time goes in v4:
time: 45.5 us; the launch traced here: 45.4 us
  Pallas kernels  44.6 us (98%)
  local copies, waits for them, and re-layouts  0.88 us (2%)
    pallas_call x1, Pallas kernels, shards(): pl.pallas_call(functools.partial(kernel, planes, gy, gz), out_shape=jax.S...  44.6 us

profile of v4, /device:TPU:1, one launch (start us, length us, event | category | flops | bytes accessed | tf_op | source)
XLA Modules:
  0.0 45.4 jit_solution(14051511688363610900)
XLA Ops:
  0.0 44.6 %project.1 = f32[3,2,32,1024]{3,2,1,0:T(8,128)S(1)} custom-call(f32[3,2,32,1024]{3,2,1,0:T(8,128)} %vel_hbm.1, f32[32]{0:T(128)} %zl_hbm.1, f32[32]{0:T(128)} %zu_hbm.1, f32[32]{0:T(128)} %zs_hbm.1, bf16[2,256,1024]{2,1,0:T(8,128)(2,1)} %constant.4.clone.ftab_hbm, bf16[2,1024,256]{2,1,0:T(8,128)(2,1)} %constant.5.clone.itab_hbm), custom_call_target="tpu_custom_call" | custom-call | tf_op jit(solution)/shard_map/project/pallas_call | solution.py:468
  44.6 0.9 %copy.8 = f32[3,2,32,1024]{3,2,1,0:T(8,128)} copy(f32[3,2,32,1024]{3,2,1,0:T(8,128)S(1)} %project.1) | data formatting | bytes 1572864

commit v5 on v4

--- a/solution.py
+++ b/solution.py
@@ -116,6 +116,13 @@
     def y_send(src, dst, ssem, rsem, f, partners):
         for g in partners:
             y_copy(src, dst, ssem, rsem, f, g).start()
+
+    def y_send_first(src, dst, ssem, rsem, f, first):
+        for t in first:
+            @pl.when(chip != t)
+            def _():
+                y_send(src, dst, ssem, rsem, f, [2 * t, 2 * t + 1])
+
 
     def y_wait_recv(src, dst, ssem, rsem, f):
         for g in y_all:
@@ -410,10 +417,26 @@
 
     tiles = [(field_re[pl.ds(s, planes, stride=8), :], field_im[pl.ds(s, planes, stride=8), :]) for s in range(8)]
     inverse(0, tiles)
-    y_send(send_b, recv_b, b_ssem, b_rsem, 0, y_all)
+    y_send_first(send_b, recv_b, b_ssem, b_rsem, 0, [0])
+    y_send_first(send_b, recv_b, b_ssem, b_rsem, 0, [1])
+    y_send_first(send_b, recv_b, b_ssem, b_rsem, 0, [2])
+    y_send_first(send_b, recv_b, b_ssem, b_rsem, 0, [3])
+    y_send_first(send_b, recv_b, b_ssem, b_rsem, 0, [4])
+    y_send_first(send_b, recv_b, b_ssem, b_rsem, 0, [5])
+    y_send_first(send_b, recv_b, b_ssem, b_rsem, 0, [6])
+    y_send_first(send_b, recv_b, b_ssem, b_rsem, 0, [7])
+    y_send(send_b, recv_b, b_ssem, b_rsem, 0, [mate])
     recv_b[0, me] = send_b[0, me]
     inverse(1, [(-ky[s:s + 1, :] * im, ky[s:s + 1, :] * re) for s, (re, im) in enumerate(tiles)])
-    y_send(send_b, recv_b, b_ssem, b_rsem, 1, y_all)
+    y_send_first(send_b, recv_b, b_ssem, b_rsem, 1, [0])
+    y_send_first(send_b, recv_b, b_ssem, b_rsem, 1, [1])
+    y_send_first(send_b, recv_b, b_ssem, b_rsem, 1, [2])
+    y_send_first(send_b, recv_b, b_ssem, b_rsem, 1, [3])
+    y_send_first(send_b, recv_b, b_ssem, b_rsem, 1, [4])
+    y_send_first(send_b, recv_b, b_ssem, b_rsem, 1, [5])
+    y_send_first(send_b, recv_b, b_ssem, b_rsem, 1, [6])
+    y_send_first(send_b, recv_b, b_ssem, b_rsem, 1, [7])
+    y_send(send_b, recv_b, b_ssem, b_rsem, 1, [mate])
     recv_b[1, me] = send_b[1, me]
 
     def unstage(f, grad):

time: 45.5 us -> 44.1 us (0.969)
  Pallas kernels: 44.6 us -> 43.1 us
    pallas_call x1, Pallas kernels: 44.6 us -> 43.1 us  [shards(): pl.pallas_call(functools.partial(kernel, planes, gy, gz), out_shape=jax.S...]
where the time goes in v5:
time: 44.1 us; the launch traced here: 44 us
  Pallas kernels  43.1 us (98%)
  local copies, waits for them, and re-layouts  0.88 us (2%)
    pallas_call x1, Pallas kernels, shards(): pl.pallas_call(functools.partial(kernel, planes, gy, gz), out_shape=jax.S...  43.1 us
    unnamed x1, local copies, waits for them, and re-layouts  0.88 us

profile of v5, /device:TPU:1, one launch (start us, length us, event | category | flops | bytes accessed | tf_op | source)
XLA Modules:
  0.0 44.0 jit_solution(9209587559533159176)
XLA Ops:
  0.0 43.1 %project.1 = f32[3,2,32,1024]{3,2,1,0:T(8,128)S(1)} custom-call(f32[3,2,32,1024]{3,2,1,0:T(8,128)} %vel_hbm.1, f32[32]{0:T(128)} %zl_hbm.1, f32[32]{0:T(128)} %zu_hbm.1, f32[32]{0:T(128)} %zs_hbm.1, bf16[2,256,1024]{2,1,0:T(8,128)(2,1)} %constant.4.clone.ftab_hbm, bf16[2,1024,256]{2,1,0:T(8,128)(2,1)} %constant.5.clone.itab_hbm), custom_call_target="tpu_custom_call" | custom-call | tf_op jit(solution)/shard_map/project/pallas_call | solution.py:491
  43.1 0.9 %copy.8 = f32[3,2,32,1024]{3,2,1,0:T(8,128)} copy(f32[3,2,32,1024]{3,2,1,0:T(8,128)S(1)} %project.1) | data formatting | bytes 1572864

commit v6 on v4

--- a/solution.py
+++ b/solution.py
@@ -39,7 +39,19 @@
         low = (values - high.astype(np.float64)).astype(ml_dtypes.bfloat16)
         return np.stack([high, low])
 
-    return split(table), split(table.T / NY)
+    t, u = np.arange(128), np.arange(256)
+    half = 4 * t
+    half[0] = NY // 2
+    m = np.concatenate([4 * t, -half, 4 * t + 2, -4 * t - 2, 4 * u + 1, -4 * u - 1]) % NY
+
+    def both(y):
+        phase = 2.0 * np.pi * ((y[:, None] * m[None, :]) % NY) / NY
+        return np.cos(phase), np.sin(phase)
+
+    r = np.arange(32)
+    edge = np.concatenate(both(64 * (r // 2) + r % 2), axis=1)
+    turn = np.stack(both(8 * (r % 8) + 2 * (r // 8))).astype(np.float32)
+    return split(table), split(table.T / NY), split(edge), turn
 
 
 def dot(a, b):
@@ -56,13 +68,13 @@
 
 def kernel(
     planes, gy, gz,
-    vel_hbm, zl_hbm, zu_hbm, zs_hbm, ftab_hbm, itab_hbm, out,
-    vel, zl, zu, zs, ftab, itab, rows_buf, send_f, recv_f, send_b, recv_b,
+    vel_hbm, zl_hbm, zu_hbm, zs_hbm, ftab_hbm, itab_hbm, etab_hbm, turn_hbm, out,
+    vel, zl, zu, zs, ftab, itab, etab, turn, edge_buf, edge_rows, edge_send, edge_recv, edge_sum, edge, rows_buf, send_f, recv_f, send_b, recv_b,
     halo_send, halo_recv, vhat, field_re, field_im,
     inv_piv, mult, ratio, beta, gamma,
     mat_all, rhs_all, red_den, red_bden, red_psi, red_b31, red_br, red_r, red_e, red_phi, red_f,
     grad, grad_q,
-    in_sem, halo_ssem, halo_rsem, f_ssem, f_rsem, b_ssem, b_rsem, m_ssem, m_rsem, r_ssem, r_rsem,
+    in_sem, e_ssem, e_rsem, halo_ssem, halo_rsem, f_ssem, f_rsem, b_ssem, b_rsem, m_ssem, m_rsem, r_ssem, r_rsem,
 ):
     me = lax.axis_index("gy")
     mz = lax.axis_index("gz")
@@ -75,6 +87,8 @@
     ]
     copy_ft = pltpu.make_async_copy(ftab_hbm, ftab, in_sem.at[6])
     copy_it = pltpu.make_async_copy(itab_hbm, itab, in_sem.at[7])
+    copy_et = pltpu.make_async_copy(etab_hbm, etab, in_sem.at[8])
+    copy_tt = pltpu.make_async_copy(turn_hbm, turn, in_sem.at[9])
     copy_in[1].start()
     copy_in[2].start()
     barrier = pltpu.get_barrier_semaphore()
@@ -95,7 +109,7 @@
         pl.semaphore_signal(barrier, inc=1, device_id={"gy": g}, device_id_type=MESH)
     for o in z_all:
         pl.semaphore_signal(barrier, inc=1, device_id={"gz": z_partner(o, 1)}, device_id_type=MESH)
-    for copy in (copy_z[2], copy_in[0], copy_z[0], copy_z[1], copy_ft, copy_it):
+    for copy in (copy_z[2], copy_in[0], copy_z[0], copy_z[1], copy_et, copy_tt, copy_ft, copy_it):
         copy.start()
 
     def stage(f, re, im):
@@ -117,6 +131,21 @@
         for g in partners:
             y_copy(src, dst, ssem, rsem, f, g).start()
 
+    def y_send_first(src, dst, ssem, rsem, f, first):
+        for t in first:
+            @pl.when(chip != t)
+            def _():
+                y_send(src, dst, ssem, rsem, f, [2 * t, 2 * t + 1])
+        for dz in Y_ORDER:
+            g = y_partner(dz, 0)
+            other = g >= 0
+            for t in first:
+                other = other & (g != 2 * t)
+
+            @pl.when(other)
+            def _():
+                y_send(src, dst, ssem, rsem, f, [g, g + 1])
+
     def y_wait_recv(src, dst, ssem, rsem, f):
         for g in y_all:
             pltpu.make_async_remote_copy(
@@ -146,14 +175,20 @@
         for o in z_all:
             z_copy(buf, ssem, rsem, o, mz).wait_send()
 
-    def halo_copies(f):
+    def edge_copy(g):
+        return pltpu.make_async_remote_copy(
+            src_ref=edge_send.at[g], dst_ref=edge_recv.at[me],
+            send_sem=e_ssem.at[g], recv_sem=e_rsem.at[me],
+            device_id={"gy": g}, device_id_type=MESH)
+
+    def halo_copies():
         up = pltpu.make_async_remote_copy(
-            src_ref=halo_send.at[f, 0], dst_ref=halo_recv.at[f, 0],
-            send_sem=halo_ssem.at[f, 0], recv_sem=halo_rsem.at[f, 0],
+            src_ref=halo_send.at[0], dst_ref=halo_recv.at[0],
+            send_sem=halo_ssem.at[0], recv_sem=halo_rsem.at[0],
             device_id={"gz": lax.rem(mz + 1, gz)}, device_id_type=MESH)
         down = pltpu.make_async_remote_copy(
-            src_ref=halo_send.at[f, 1], dst_ref=halo_recv.at[f, 1],
-            send_sem=halo_ssem.at[f, 1], recv_sem=halo_rsem.at[f, 1],
+            src_ref=halo_send.at[1], dst_ref=halo_recv.at[1],
+            send_sem=halo_ssem.at[1], recv_sem=halo_rsem.at[1],
             device_id={"gz": lax.rem(mz + gz - 1, gz)}, device_id_type=MESH)
         return up, down
 
@@ -167,38 +202,45 @@
 
     kx_lane = (lax.broadcasted_iota(jnp.int32, (1, NY), 1) % KX + 1).astype(f32)
 
-    def slope_diff(values, f, part, slope_wide):
-        low = jnp.where(mz > 0, halo_recv[f, 0, part:part + 1, :], 0.0)
-        high = jnp.where(mz < gz - 1, halo_recv[f, 1, part:part + 1, :], 0.0)
+    def slope_diff(values, low, high):
         above = jnp.concatenate([values[1:], high], axis=0)
         below = jnp.concatenate([low, values[:-1]], axis=0)
         return slope_wide * (above - below)
 
+    copy_z[2].wait()
+    slope = column(zs)
+    slope_wide = jnp.concatenate([slope] * 8, axis=1)
+    nothing = jnp.zeros((1, NY), f32)
     copy_in[1].wait()
     stage(1, vel[1, 0], vel[1, 1])
     copy_in[2].wait()
-    for part in range(2):
-        halo_send[0, 0, part:part + 1, :] = vel[2, part, planes - 1:planes, :]
-        halo_send[0, 1, part:part + 1, :] = vel[2, part, 0:1, :]
+    for t in range(8):
+        for part in range(2):
+            for e, k in enumerate((0, planes - 1)):
+                r = 4 * t + 2 * part + e
+                edge_rows[r:r + 1, :] = vel[2, part, k:k + 1, t * 128:t * 128 + 128]
+    edge_buf[...] = jnp.zeros((LANES, LANES), f32)
+    for q in range(4):
+        edge_buf[q * 32:q * 32 + 32, :32] = edge_rows[:, q * 32:q * 32 + 32]
+    edge_rows[...] = edge_buf[...].T[:32]
+    for j in range(KX):
+        edge_send[j] = edge_rows[pl.ds(j, 2, stride=16), :]
+    copy_in[0].wait()
+    stage(
+        0,
+        slope_diff(vel[2, 0], nothing, nothing) - kx_lane * vel[0, 1],
+        slope_diff(vel[2, 1], nothing, nothing) + kx_lane * vel[0, 0],
+    )
     pl.semaphore_wait(barrier, len(y_all) + len(Z_ORDER))
-    halo_w = halo_copies(0)
-    halo_w[0].start()
-    halo_w[1].start()
     to_core = [[y_partner(dz, c) for dz in Y_ORDER] for c in range(2)]
-    y_send(send_f, recv_f, f_ssem, f_rsem, 1, to_core[0] + [mate] + to_core[1][:4])
-    recv_f[1, me] = send_f[1, me]
-
-    copy_z[2].wait()
-    slope = column(zs)
-    slope_wide = jnp.concatenate([slope] * 8, axis=1)
-    copy_in[0].wait()
-    halo_w[0].wait_recv()
-    halo_w[1].wait_recv()
-    stage(0, slope_diff(vel[2, 0], 0, 0, slope_wide) - kx_lane * vel[0, 1], slope_diff(vel[2, 1], 0, 1, slope_wide) + kx_lane * vel[0, 0])
-    y_send(send_f, recv_f, f_ssem, f_rsem, 0, to_core[0] + [mate])
-    y_send(send_f, recv_f, f_ssem, f_rsem, 1, to_core[1][4:])
-    y_send(send_f, recv_f, f_ssem, f_rsem, 0, to_core[1])
-    recv_f[0, me] = send_f[0, me]
+    for partners in (to_core[0] + [mate], to_core[1]):
+        for g in partners:
+            edge_copy(g).start()
+        y_send(send_f, recv_f, f_ssem, f_rsem, 1, partners)
+        y_send(send_f, recv_f, f_ssem, f_rsem, 0, partners)
+    for f in range(2):
+        recv_f[f, me] = send_f[f, me]
+    edge_recv[me] = edge_send[me]
 
     copy_z[0].wait()
     copy_z[1].wait()
@@ -289,6 +331,28 @@
         ky_row = ky[s:s + 1, :]
         vhat[s, 0] = -ky_row * im
         vhat[s, 1] = ky_row * re
+    copy_et.wait()
+    copy_tt.wait()
+    for g in y_all:
+        pltpu.make_async_remote_copy(
+            src_ref=edge_send.at[g], dst_ref=edge_recv.at[g],
+            send_sem=e_ssem.at[g], recv_sem=e_rsem.at[g],
+            device_id={"gy": g}, device_id_type=MESH).wait_recv()
+    for d in range(gy):
+        edge_buf[2 * d:2 * d + 2, :] = edge_recv[d]
+    partial = product(edge_buf[...].T[:, :32], etab[0], etab[1])
+    for s in range(16):
+        edge_sum[s] = partial[:, s * 128:s * 128 + 128]
+    for s in range(8):
+        cos, sin = turn[0, :, s * 128:s * 128 + 128], turn[1, :, s * 128:s * 128 + 128]
+        for e in range(2):
+            rc, rs, ic, is_ = (
+                edge_sum[s + off, pl.ds(part + e, 32, stride=4), :] for part in (0, 2) for off in (0, 8))
+            re, im = rc + is_, ic - rs
+            edge[e, 0, s:s + 1, :] = jnp.sum(re * cos + im * sin, axis=0, keepdims=True)
+            edge[e, 1, s:s + 1, :] = jnp.sum(im * cos - re * sin, axis=0, keepdims=True)
+    below = jnp.full((8, LANES), zs[0]) / jnp.full((8, LANES), zl[0])
+    above = jnp.full((8, LANES), zs[planes - 1]) / jnp.full((8, LANES), zu[planes - 1])
     y_wait_recv(send_f, recv_f, f_ssem, f_rsem, 0)
     for s, (re, im) in enumerate(forward(0)):
         field_re[pl.ds(s, planes, stride=8), :] = re + vhat[s, 0]
@@ -316,10 +380,10 @@
         return ar, ai
 
     ar, ai = lax.fori_loop(0, planes, back, (zero, zero), unroll=True)
-    rhs_all[mz, 0] = ar
-    rhs_all[mz, 1] = ai
-    rhs_all[mz, 2] = field_re[last, :]
-    rhs_all[mz, 3] = field_im[last, :]
+    rhs_all[mz, 0] = ar - below * edge[0, 0]
+    rhs_all[mz, 1] = ai - below * edge[0, 1]
+    rhs_all[mz, 2] = field_re[last, :] + above * edge[1, 0]
+    rhs_all[mz, 3] = field_im[last, :] + above * edge[1, 1]
     z_send(rhs_all, r_ssem, r_rsem)
 
     z_wait_recv(mat_all, m_ssem, m_rsem)
@@ -410,10 +474,12 @@
 
     tiles = [(field_re[pl.ds(s, planes, stride=8), :], field_im[pl.ds(s, planes, stride=8), :]) for s in range(8)]
     inverse(0, tiles)
-    y_send(send_b, recv_b, b_ssem, b_rsem, 0, y_all)
+    y_send_first(send_b, recv_b, b_ssem, b_rsem, 0, (0, 1, 2))
+    y_send(send_b, recv_b, b_ssem, b_rsem, 0, [mate])
     recv_b[0, me] = send_b[0, me]
     inverse(1, [(-ky[s:s + 1, :] * im, ky[s:s + 1, :] * re) for s, (re, im) in enumerate(tiles)])
-    y_send(send_b, recv_b, b_ssem, b_rsem, 1, y_all)
+    y_send_first(send_b, recv_b, b_ssem, b_rsem, 1, (0, 1, 2))
+    y_send(send_b, recv_b, b_ssem, b_rsem, 1, [mate])
     recv_b[1, me] = send_b[1, me]
 
     def unstage(f, grad):
@@ -426,8 +492,8 @@
                     first = h * 64 + part * 32
                     grad[part, :, h * 512 + c * 128:h * 512 + c * 128 + 128] = block[first:first + 32]
 
-    for copy in halo_w:
-        copy.wait_send()
+    for g in y_all:
+        edge_copy(g).wait_send()
     for f in range(2):
         y_wait_send(send_f, recv_f, f_ssem, f_rsem, f)
     z_wait_send(mat_all, m_ssem, m_rsem)
@@ -435,9 +501,9 @@
     y_wait_recv(send_b, recv_b, b_ssem, b_rsem, 0)
     unstage(0, grad)
     for part in range(2):
-        halo_send[1, 0, part:part + 1, :] = grad[part, planes - 1:planes, :]
-        halo_send[1, 1, part:part + 1, :] = grad[part, 0:1, :]
-    halo_p = halo_copies(1)
+        halo_send[0, part:part + 1, :] = grad[part, planes - 1:planes, :]
+        halo_send[1, part:part + 1, :] = grad[part, 0:1, :]
+    halo_p = halo_copies()
     halo_p[0].start()
     halo_p[1].start()
     out[0, 0] = vel[0, 0] + kx_lane * grad[1]
@@ -450,7 +516,9 @@
     halo_p[0].wait_recv()
     halo_p[1].wait_recv()
     for part in range(2):
-        out[2, part] = vel[2, part] - slope_diff(grad[part], 1, part, slope_wide)
+        low = jnp.where(mz > 0, halo_recv[0, part:part + 1, :], 0.0)
+        high = jnp.where(mz < gz - 1, halo_recv[1, part:part + 1, :], 0.0)
+        out[2, part] = vel[2, part] - slope_diff(grad[part], low, high)
 
     for copy in halo_p:
         copy.wait_send()
@@ -460,7 +528,7 @@
 def shards(velocity, z_lower, z_upper, z_slope):
     gy, gz = lax.axis_size("gy"), lax.axis_size("gz")
     planes = velocity.shape[2]
-    ftab, itab = (jnp.asarray(table) for table in fourier_tables())
+    ftab, itab, etab, turn = (jnp.asarray(table) for table in fourier_tables())
     f32 = jnp.float32
     hbm = pl.BlockSpec(memory_space=pl.ANY)
     lines = (planes * 8, LANES)
@@ -468,7 +536,7 @@
     return pl.pallas_call(
         functools.partial(kernel, planes, gy, gz),
         out_shape=jax.ShapeDtypeStruct(velocity.shape, f32),
-        in_specs=[pl.BlockSpec(memory_space=pltpu.HBM)] * 6,
+        in_specs=[pl.BlockSpec(memory_space=pltpu.HBM)] * 8,
         out_specs=pl.BlockSpec(memory_space=pltpu.VMEM),
         scratch_shapes=[
             pltpu.VMEM(velocity.shape, f32),
@@ -477,13 +545,21 @@
             pltpu.SMEM((planes,), f32),
             pltpu.VMEM(ftab.shape, jnp.bfloat16),
             pltpu.VMEM(itab.shape, jnp.bfloat16),
+            pltpu.VMEM(etab.shape, jnp.bfloat16),
+            pltpu.VMEM(turn.shape, f32),
+            pltpu.VMEM((LANES, LANES), f32),
+            pltpu.VMEM((32, LANES), f32),
+            pltpu.VMEM((gy, 2, LANES), f32),
+            pltpu.VMEM((gy, 2, LANES), f32),
+            pltpu.VMEM((16, LANES, LANES), f32),
+            pltpu.VMEM((2, 2, 8, LANES), f32),
             pltpu.VMEM((512, LANES), f32),
             pltpu.VMEM((2, gy, 32, LANES), f32),
             pltpu.VMEM((2, gy, 32, LANES), f32),
             pltpu.VMEM((2, gy, 32, LANES), f32),
             pltpu.VMEM((2, gy, 32, LANES), f32),
-            pltpu.VMEM((2, 2, 2, NY), f32),
-            pltpu.VMEM((2, 2, 2, NY), f32),
+            pltpu.VMEM((2, 2, NY), f32),
+            pltpu.VMEM((2, 2, NY), f32),
             pltpu.VMEM((8, 2, planes, LANES), f32),
             pltpu.VMEM(lines, f32),
             pltpu.VMEM(lines, f32),
@@ -505,7 +581,7 @@
             pltpu.VMEM((gz + 1, 2, 8, LANES), f32),
             pltpu.VMEM((2, planes, NY), f32),
             pltpu.VMEM((2, planes, NY), f32),
-            dma((8,)), dma((2, 2)), dma((2, 2)),
+            dma((10,)), dma((gy,)), dma((gy,)), dma((2,)), dma((2,)),
             dma((2, gy)), dma((2, gy)), dma((2, gy)), dma((2, gy)),
             dma((gz,)), dma((gz,)), dma((gz,)), dma((gz,)),
         ],
@@ -513,7 +589,7 @@
             collective_id=0, has_side_effects=True, vmem_limit_bytes=40 * 1024 * 1024
         ),
         name="project",
-    )(*(pltpu.with_memory_space_constraint(a, pltpu.HBM) for a in (velocity, z_lower, z_upper, z_slope, ftab, itab)))
+    )(*(pltpu.with_memory_space_constraint(a, pltpu.HBM) for a in (velocity, z_lower, z_upper, z_slope, ftab, itab, etab, turn)))
 
 
 def solution(mesh):

time: 45.5 us -> 43.5 us (0.956)
  Pallas kernels: 44.6 us -> 42.5 us
    pallas_call x1, Pallas kernels: 44.6 us -> 42.5 us  [shards(): pl.pallas_call(functools.partial(kernel, planes, gy, gz), out_shape=jax.S...]
where the time goes in v6:
time: 43.5 us; the launch traced here: 43.4 us
  Pallas kernels  42.5 us (98%)
  local copies, waits for them, and re-layouts  0.88 us (2%)
    pallas_call x1, Pallas kernels, shards(): pl.pallas_call(functools.partial(kernel, planes, gy, gz), out_shape=jax.S...  42.5 us
    unnamed x1, local copies, waits for them, and re-layouts  0.88 us

profile of v6, /device:TPU:1, one launch (start us, length us, event | category | flops | bytes accessed | tf_op | source)
XLA Modules:
  0.0 43.4 jit_solution(9184235220001239424)
XLA Ops:
  0.0 42.5 %project.1 = f32[3,2,32,1024]{3,2,1,0:T(8,128)S(1)} custom-call(f32[3,2,32,1024]{3,2,1,0:T(8,128)} %vel_hbm.1, f32[32]{0:T(128)} %zl_hbm.1, f32[32]{0:T(128)} %zu_hbm.1, f32[32]{0:T(128)} %zs_hbm.1, bf16[2,256,1024]{2,1,0:T(8,128)(2,1)} %constant.8.clone.ftab_hbm, bf16[2,1024,256]{2,1,0:T(8,128)(2,1)} %constant.9.clone.itab_hbm, ...), custom_call_target="tpu_custom_call" | custom-call | tf_op jit(solution)/shard_map/project/pallas_call | solution.py:536
  42.5 0.9 %copy.10 = f32[3,2,32,1024]{3,2,1,0:T(8,128)} copy(f32[3,2,32,1024]{3,2,1,0:T(8,128)S(1)} %project.1) | data formatting | bytes 1572864

commit v7 on v6

--- a/solution.py
+++ b/solution.py
@@ -71,7 +71,7 @@
     vel_hbm, zl_hbm, zu_hbm, zs_hbm, ftab_hbm, itab_hbm, etab_hbm, turn_hbm, out,
     vel, zl, zu, zs, ftab, itab, etab, turn, edge_buf, edge_rows, edge_send, edge_recv, edge_sum, edge, rows_buf, send_f, recv_f, send_b, recv_b,
     halo_send, halo_recv, vhat, field_re, field_im,
-    inv_piv, mult, ratio, beta, gamma,
+    inv_piv, mult, ratio, beta, gamma, low_row, high_row,
     mat_all, rhs_all, red_den, red_bden, red_psi, red_b31, red_br, red_r, red_e, red_phi, red_f,
     grad, grad_q,
     in_sem, e_ssem, e_rsem, halo_ssem, halo_rsem, f_ssem, f_rsem, b_ssem, b_rsem, m_ssem, m_rsem, r_ssem, r_rsem,
@@ -221,8 +221,8 @@
                 edge_rows[r:r + 1, :] = vel[2, part, k:k + 1, t * 128:t * 128 + 128]
     edge_buf[...] = jnp.zeros((LANES, LANES), f32)
     for q in range(4):
-        edge_buf[q * 32:q * 32 + 32, :32] = edge_rows[:, q * 32:q * 32 + 32]
-    edge_rows[...] = edge_buf[...].T[:32]
+        edge_buf[q * 32:q * 32 + 32, :32] = edge_rows[:32, q * 32:q * 32 + 32]
+    edge_rows[:32, :] = edge_buf[...].T[:32]
     for j in range(KX):
         edge_send[j] = edge_rows[pl.ds(j, 2, stride=16), :]
     copy_in[0].wait()
@@ -275,16 +275,22 @@
     lax.fori_loop(0, planes, factor, (zero, one_v))
 
     def unfold(i, state):
-        b, g = state
+        b, g, width = state
         k = planes - 1 - i
         r = ratio[rows_of(k), :]
         b = beta[rows_of(k), :] - r * b
         g = -r * g
         beta[rows_of(k), :] = b
         gamma[rows_of(k), :] = g
-        return b, g
-
-    b0, g0 = lax.fori_loop(0, planes, unfold, (zero, one_v))
+        low_row[rows_of(k), :] = b * width
+        high_row[rows_of(k), :] = g * width
+        before = jnp.maximum(k - 1, 0)
+        wider = width * (jnp.full((8, LANES), zl[k]) / jnp.full((8, LANES), zu[before]))
+        return b, g, jnp.where(k > 0, wider, width)
+
+    b0, g0, first_width = lax.fori_loop(0, planes, unfold, (zero, one_v, one_v))
+    low_scale = -1.0 / (jnp.full((8, LANES), zl[0]) * first_width)
+    high_scale = -1.0 / jnp.full((8, LANES), zu[planes - 1])
     last = slice((planes - 1) * 8, planes * 8)
     mat_all[mz, 0] = b0
     mat_all[mz, 1] = g0
@@ -358,6 +364,19 @@
         field_re[pl.ds(s, planes, stride=8), :] = re + vhat[s, 0]
         field_im[pl.ds(s, planes, stride=8), :] = im + vhat[s, 1]
 
+    sums = [[zero] * 4 for _ in range(4)]
+    for k in range(planes):
+        rows = slice(k * 8, k * 8 + 8)
+        re, im, low, high = field_re[rows, :], field_im[rows, :], low_row[rows, :], high_row[rows, :]
+        for n, term in enumerate((low * re, low * im, high * re, high * im)):
+            sums[n][k % 4] = sums[n][k % 4] + term
+    lr, li, hr, hi = ((t[0] + t[1]) + (t[2] + t[3]) for t in sums)
+    rhs_all[mz, 0] = low_scale * lr - below * edge[0, 0]
+    rhs_all[mz, 1] = low_scale * li - below * edge[0, 1]
+    rhs_all[mz, 2] = high_scale * hr + above * edge[1, 0]
+    rhs_all[mz, 3] = high_scale * hi + above * edge[1, 1]
+    z_send(rhs_all, r_ssem, r_rsem)
+
     def down(k, state):
         sr, si = state
         inverse, m = inv_piv[rows_of(k), :], mult[rows_of(k), :]
@@ -379,12 +398,7 @@
         field_im[rows_of(k), :] = ai
         return ar, ai
 
-    ar, ai = lax.fori_loop(0, planes, back, (zero, zero), unroll=True)
-    rhs_all[mz, 0] = ar - below * edge[0, 0]
-    rhs_all[mz, 1] = ai - below * edge[0, 1]
-    rhs_all[mz, 2] = field_re[last, :] + above * edge[1, 0]
-    rhs_all[mz, 3] = field_im[last, :] + above * edge[1, 1]
-    z_send(rhs_all, r_ssem, r_rsem)
+    lax.fori_loop(0, planes, back, (zero, zero), unroll=True)
 
     z_wait_recv(mat_all, m_ssem, m_rsem)
     red_r[0] = zero
@@ -398,7 +412,8 @@
         red_den[d] = den
         red_bden[d] = mat_all[d, 0] * den
         red_psi[d] = psi
-        red_br[d] = br
+        red_b31[d] = mat_all[d, 2] + br * (mat_all[d, 0] * den)
+        red_br[d] = br * den
         r = mat_all[d, 3] + br * psi
         red_r[d + 1] = r
         return r
@@ -408,13 +423,11 @@
 
     def reduce_rhs(d, state):
         er, ei = state
-        den, bden, br, b31 = red_den[d], red_bden[d], red_br[d], mat_all[d, 2]
-        pr = den * rhs_all[d, 0] + bden * er
-        pi = den * rhs_all[d, 1] + bden * ei
-        er = rhs_all[d, 2] + b31 * er + br * pr
-        ei = rhs_all[d, 3] + b31 * ei + br * pi
-        red_phi[d, 0] = pr
-        red_phi[d, 1] = pi
+        den, bden, brden, step = red_den[d], red_bden[d], red_br[d], red_b31[d]
+        red_phi[d, 0] = den * rhs_all[d, 0] + bden * er
+        red_phi[d, 1] = den * rhs_all[d, 1] + bden * ei
+        er = (rhs_all[d, 2] + brden * rhs_all[d, 0]) + step * er
+        ei = (rhs_all[d, 3] + brden * rhs_all[d, 1]) + step * ei
         red_e[d + 1, 0] = er
         red_e[d + 1, 1] = ei
         return er, ei
@@ -531,7 +544,7 @@
     ftab, itab, etab, turn = (jnp.asarray(table) for table in fourier_tables())
     f32 = jnp.float32
     hbm = pl.BlockSpec(memory_space=pl.ANY)
-    lines = (planes * 8, LANES)
+    lines = (planes * 8 + 8, LANES)
     dma = pltpu.SemaphoreType.DMA
     return pl.pallas_call(
         functools.partial(kernel, planes, gy, gz),
@@ -548,19 +561,21 @@
             pltpu.VMEM(etab.shape, jnp.bfloat16),
             pltpu.VMEM(turn.shape, f32),
             pltpu.VMEM((LANES, LANES), f32),
-            pltpu.VMEM((32, LANES), f32),
+            pltpu.VMEM((160, LANES), f32),
             pltpu.VMEM((gy, 2, LANES), f32),
             pltpu.VMEM((gy, 2, LANES), f32),
             pltpu.VMEM((16, LANES, LANES), f32),
-            pltpu.VMEM((2, 2, 8, LANES), f32),
-            pltpu.VMEM((512, LANES), f32),
+            pltpu.VMEM((3, 2, 8, LANES), f32),
+            pltpu.VMEM((528, LANES), f32),
             pltpu.VMEM((2, gy, 32, LANES), f32),
             pltpu.VMEM((2, gy, 32, LANES), f32),
             pltpu.VMEM((2, gy, 32, LANES), f32),
             pltpu.VMEM((2, gy, 32, LANES), f32),
-            pltpu.VMEM((2, 2, NY), f32),
-            pltpu.VMEM((2, 2, NY), f32),
+            pltpu.VMEM((4, 2, NY), f32),
+            pltpu.VMEM((4, 2, NY), f32),
             pltpu.VMEM((8, 2, planes, LANES), f32),
+            pltpu.VMEM(lines, f32),
+            pltpu.VMEM(lines, f32),
             pltpu.VMEM(lines, f32),
             pltpu.VMEM(lines, f32),
             pltpu.VMEM(lines, f32),

time: 43.5 us -> 43.4 us (level)
  no operation moved by 1% of the time
where the time goes in v7:
time: 43.4 us; the launch traced here: 43.2 us
  Pallas kernels  42.3 us (97%)
  local copies, waits for them, and re-layouts  0.88 us (2%)
    pallas_call x1, Pallas kernels, shards(): pl.pallas_call(functools.partial(kernel, planes, gy, gz), out_shape=jax.S...  42.3 us
    unnamed x1, local copies, waits for them, and re-layouts  0.88 us

profile of v7, /device:TPU:1, one launch (start us, length us, event | category | flops | bytes accessed | tf_op | source)
XLA Modules:
  0.0 43.2 jit_solution(13449290806269939703)
XLA Ops:
  0.0 42.3 %project.1 = f32[3,2,32,1024]{3,2,1,0:T(8,128)S(1)} custom-call(f32[3,2,32,1024]{3,2,1,0:T(8,128)} %vel_hbm.1, f32[32]{0:T(128)} %zl_hbm.1, f32[32]{0:T(128)} %zu_hbm.1, f32[32]{0:T(128)} %zs_hbm.1, bf16[2,256,1024]{2,1,0:T(8,128)(2,1)} %constant.8.clone.ftab_hbm, bf16[2,1024,256]{2,1,0:T(8,128)(2,1)} %constant.9.clone.itab_hbm, ...), custom_call_target="tpu_custom_call" | custom-call | tf_op jit(solution)/shard_map/project/pallas_call | solution.py:549
  42.3 0.9 %copy.10 = f32[3,2,32,1024]{3,2,1,0:T(8,128)} copy(f32[3,2,32,1024]{3,2,1,0:T(8,128)S(1)} %project.1) | data formatting | bytes 1572864

commit v8 on v7

--- a/solution.py
+++ b/solution.py
@@ -124,7 +124,7 @@
     def y_copy(src, dst, ssem, rsem, f, g):
         return pltpu.make_async_remote_copy(
             src_ref=src.at[f, g], dst_ref=dst.at[f, me],
-            send_sem=ssem.at[f, g], recv_sem=rsem.at[f, me],
+            send_sem=ssem.at[f], recv_sem=rsem.at[f],
             device_id={"gy": g}, device_id_type=MESH)
 
     def y_send(src, dst, ssem, rsem, f, partners):
@@ -146,40 +146,43 @@
             def _():
                 y_send(src, dst, ssem, rsem, f, [g, g + 1])
 
+    def y_all_copy(src, dst, ssem, rsem, f):
+        rest = pl.ds(0, gy - 1)
+        return pltpu.make_async_remote_copy(
+            src_ref=src.at[f, rest], dst_ref=dst.at[f, rest], send_sem=ssem.at[f], recv_sem=rsem.at[f],
+            device_id={"gy": mate}, device_id_type=MESH)
+
     def y_wait_recv(src, dst, ssem, rsem, f):
-        for g in y_all:
-            pltpu.make_async_remote_copy(
-                src_ref=src.at[f, g], dst_ref=dst.at[f, g],
-                send_sem=ssem.at[f, g], recv_sem=rsem.at[f, g],
-                device_id={"gy": g}, device_id_type=MESH).wait_recv()
+        y_all_copy(src, dst, ssem, rsem, f).wait_recv()
 
     def y_wait_send(src, dst, ssem, rsem, f):
-        for g in y_all:
-            y_copy(src, dst, ssem, rsem, f, g).wait_send()
-
-    def z_copy(buf, ssem, rsem, o, slot):
+        y_all_copy(src, dst, ssem, rsem, f).wait_send()
+
+    def z_copy(buf, ssem, rsem, g, slots):
         return pltpu.make_async_remote_copy(
-            src_ref=buf.at[slot], dst_ref=buf.at[slot],
-            send_sem=ssem.at[o], recv_sem=rsem.at[o],
-            device_id={"gz": z_partner(o, 1)}, device_id_type=MESH)
+            src_ref=buf.at[slots], dst_ref=buf.at[slots], send_sem=ssem, recv_sem=rsem,
+            device_id={"gz": g}, device_id_type=MESH)
 
     def z_send(buf, ssem, rsem):
         for o in z_all:
-            z_copy(buf, ssem, rsem, o, mz).start()
+            z_copy(buf, ssem, rsem, z_partner(o, 1), mz).start()
 
     def z_wait_recv(buf, ssem, rsem):
-        for o in z_all:
-            z_copy(buf, ssem, rsem, o, z_partner(o, -1)).wait_recv()
+        z_copy(buf, ssem, rsem, z_partner(0, 1), pl.ds(0, gz - 1)).wait_recv()
 
     def z_wait_send(buf, ssem, rsem):
-        for o in z_all:
-            z_copy(buf, ssem, rsem, o, mz).wait_send()
+        z_copy(buf, ssem, rsem, z_partner(0, 1), pl.ds(0, gz - 1)).wait_send()
 
     def edge_copy(g):
         return pltpu.make_async_remote_copy(
-            src_ref=edge_send.at[g], dst_ref=edge_recv.at[me],
-            send_sem=e_ssem.at[g], recv_sem=e_rsem.at[me],
+            src_ref=edge_send.at[g], dst_ref=edge_recv.at[me], send_sem=e_ssem, recv_sem=e_rsem,
             device_id={"gy": g}, device_id_type=MESH)
+
+    def edge_all_copy():
+        rest = pl.ds(0, gy - 1)
+        return pltpu.make_async_remote_copy(
+            src_ref=edge_send.at[rest], dst_ref=edge_recv.at[rest], send_sem=e_ssem, recv_sem=e_rsem,
+            device_id={"gy": mate}, device_id_type=MESH)
 
     def halo_copies():
         up = pltpu.make_async_remote_copy(
@@ -339,11 +342,7 @@
         vhat[s, 1] = ky_row * re
     copy_et.wait()
     copy_tt.wait()
-    for g in y_all:
-        pltpu.make_async_remote_copy(
-            src_ref=edge_send.at[g], dst_ref=edge_recv.at[g],
-            send_sem=e_ssem.at[g], recv_sem=e_rsem.at[g],
-            device_id={"gy": g}, device_id_type=MESH).wait_recv()
+    edge_all_copy().wait_recv()
     for d in range(gy):
         edge_buf[2 * d:2 * d + 2, :] = edge_recv[d]
     partial = product(edge_buf[...].T[:, :32], etab[0], etab[1])
@@ -505,8 +504,7 @@
                     first = h * 64 + part * 32
                     grad[part, :, h * 512 + c * 128:h * 512 + c * 128 + 128] = block[first:first + 32]
 
-    for g in y_all:
-        edge_copy(g).wait_send()
+    edge_all_copy().wait_send()
     for f in range(2):
         y_wait_send(send_f, recv_f, f_ssem, f_rsem, f)
     z_wait_send(mat_all, m_ssem, m_rsem)
@@ -596,9 +594,9 @@
             pltpu.VMEM((gz + 1, 2, 8, LANES), f32),
             pltpu.VMEM((2, planes, NY), f32),
             pltpu.VMEM((2, planes, NY), f32),
-            dma((10,)), dma((gy,)), dma((gy,)), dma((2,)), dma((2,)),
-            dma((2, gy)), dma((2, gy)), dma((2, gy)), dma((2, gy)),
-            dma((gz,)), dma((gz,)), dma((gz,)), dma((gz,)),
+            dma((10,)), dma, dma, dma((2,)), dma((2,)),
+            dma((2,)), dma((2,)), dma((2,)), dma((2,)),
+            dma, dma, dma, dma,
         ],
         compiler_params=pltpu.CompilerParams(
             collective_id=0, has_side_effects=True, vmem_limit_bytes=40 * 1024 * 1024

time: 43.4 us -> 41.4 us (0.954)
  Pallas kernels: 42.3 us -> 40.3 us
    pallas_call x1, Pallas kernels: 42.3 us -> 40.3 us  [shards(): pl.pallas_call(functools.partial(kernel, planes, gy, gz), out_shape=jax.S...]
where the time goes in v8:
time: 41.4 us; the launch traced here: 41.2 us
  Pallas kernels  40.3 us (97%)
  local copies, waits for them, and re-layouts  0.88 us (2%)
    pallas_call x1, Pallas kernels, shards(): pl.pallas_call(functools.partial(kernel, planes, gy, gz), out_shape=jax.S...  40.3 us
    unnamed x1, local copies, waits for them, and re-layouts  0.88 us

profile of v8, /device:TPU:1, one launch (start us, length us, event | category | flops | bytes accessed | tf_op | source)
XLA Modules:
  0.0 41.2 jit_solution(13672677941566314139)
XLA Ops:
  0.0 40.3 %project.1 = f32[3,2,32,1024]{3,2,1,0:T(8,128)S(1)} custom-call(f32[3,2,32,1024]{3,2,1,0:T(8,128)} %vel_hbm.1, f32[32]{0:T(128)} %zl_hbm.1, f32[32]{0:T(128)} %zu_hbm.1, f32[32]{0:T(128)} %zs_hbm.1, bf16[2,256,1024]{2,1,0:T(8,128)(2,1)} %constant.8.clone.ftab_hbm, bf16[2,1024,256]{2,1,0:T(8,128)(2,1)} %constant.9.clone.itab_hbm, ...), custom_call_target="tpu_custom_call" | custom-call | tf_op jit(solution)/shard_map/project/pallas_call | solution.py:547
  40.3 0.9 %copy.10 = f32[3,2,32,1024]{3,2,1,0:T(8,128)} copy(f32[3,2,32,1024]{3,2,1,0:T(8,128)S(1)} %project.1) | data formatting | bytes 1572864

commit v9 on v8

--- a/solution.py
+++ b/solution.py
@@ -237,9 +237,9 @@
     pl.semaphore_wait(barrier, len(y_all) + len(Z_ORDER))
     to_core = [[y_partner(dz, c) for dz in Y_ORDER] for c in range(2)]
     for partners in (to_core[0] + [mate], to_core[1]):
+        y_send(send_f, recv_f, f_ssem, f_rsem, 1, partners)
         for g in partners:
             edge_copy(g).start()
-        y_send(send_f, recv_f, f_ssem, f_rsem, 1, partners)
         y_send(send_f, recv_f, f_ssem, f_rsem, 0, partners)
     for f in range(2):
         recv_f[f, me] = send_f[f, me]

time: 41.4 us -> 41.6 us (level)
  no operation moved by 1% of the time
where the time goes in v9:
time: 41.6 us; the launch traced here: 41.3 us
  Pallas kernels  40.4 us (97%)
  local copies, waits for them, and re-layouts  0.88 us (2%)
    pallas_call x1, Pallas kernels, shards(): pl.pallas_call(functools.partial(kernel, planes, gy, gz), out_shape=jax.S...  40.4 us
    unnamed x1, local copies, waits for them, and re-layouts  0.88 us

profile of v9, /device:TPU:1, one launch (start us, length us, event | category | flops | bytes accessed | tf_op | source)
XLA Modules:
  0.0 41.3 jit_solution(17926163393713082778)
XLA Ops:
  0.0 40.4 %project.1 = f32[3,2,32,1024]{3,2,1,0:T(8,128)S(1)} custom-call(f32[3,2,32,1024]{3,2,1,0:T(8,128)} %vel_hbm.1, f32[32]{0:T(128)} %zl_hbm.1, f32[32]{0:T(128)} %zu_hbm.1, f32[32]{0:T(128)} %zs_hbm.1, bf16[2,256,1024]{2,1,0:T(8,128)(2,1)} %constant.8.clone.ftab_hbm, bf16[2,1024,256]{2,1,0:T(8,128)(2,1)} %constant.9.clone.itab_hbm, ...), custom_call_target="tpu_custom_call" | custom-call | tf_op jit(solution)/shard_map/project/pallas_call | solution.py:547
  40.4 0.9 %copy.10 = f32[3,2,32,1024]{3,2,1,0:T(8,128)} copy(f32[3,2,32,1024]{3,2,1,0:T(8,128)S(1)} %project.1) | data formatting | bytes 1572864

commit v10 on v8

--- a/solution.py
+++ b/solution.py
@@ -520,6 +520,9 @@
     out[0, 0] = vel[0, 0] + kx_lane * grad[1]
     out[0, 1] = vel[0, 1] - kx_lane * grad[0]
     y_wait_send(send_b, recv_b, b_ssem, b_rsem, 0)
+    for copy in halo_p:
+        copy.wait_send()
+    y_wait_send(send_b, recv_b, b_ssem, b_rsem, 1)
     y_wait_recv(send_b, recv_b, b_ssem, b_rsem, 1)
     unstage(1, grad_q)
     for part in range(2):
@@ -530,10 +533,6 @@
         low = jnp.where(mz > 0, halo_recv[0, part:part + 1, :], 0.0)
         high = jnp.where(mz < gz - 1, halo_recv[1, part:part + 1, :], 0.0)
         out[2, part] = vel[2, part] - slope_diff(grad[part], low, high)
-
-    for copy in halo_p:
-        copy.wait_send()
-    y_wait_send(send_b, recv_b, b_ssem, b_rsem, 1)
 
 
 def shards(velocity, z_lower, z_upper, z_slope):

time: 41.4 us -> 41.4 us (level)
  no operation moved by 1% of the time
where the time goes in v10:
time: 41.4 us; the launch traced here: 41.2 us
  Pallas kernels  40.3 us (97%)
  local copies, waits for them, and re-layouts  0.88 us (2%)
    pallas_call x1, Pallas kernels, shards(): pl.pallas_call(functools.partial(kernel, planes, gy, gz), out_shape=jax.S...  40.3 us
    unnamed x1, local copies, waits for them, and re-layouts  0.88 us

profile of v10, /device:TPU:1, one launch (start us, length us, event | category | flops | bytes accessed | tf_op | source)
XLA Modules:
  0.0 41.2 jit_solution(11505425386822973274)
XLA Ops:
  0.0 40.3 %project.1 = f32[3,2,32,1024]{3,2,1,0:T(8,128)S(1)} custom-call(f32[3,2,32,1024]{3,2,1,0:T(8,128)} %vel_hbm.1, f32[32]{0:T(128)} %zl_hbm.1, f32[32]{0:T(128)} %zu_hbm.1, f32[32]{0:T(128)} %zs_hbm.1, bf16[2,256,1024]{2,1,0:T(8,128)(2,1)} %constant.8.clone.ftab_hbm, bf16[2,1024,256]{2,1,0:T(8,128)(2,1)} %constant.9.clone.itab_hbm, ...), custom_call_target="tpu_custom_call" | custom-call | tf_op jit(solution)/shard_map/project/pallas_call | solution.py:546
  40.3 0.9 %copy.10 = f32[3,2,32,1024]{3,2,1,0:T(8,128)} copy(f32[3,2,32,1024]{3,2,1,0:T(8,128)S(1)} %project.1) | data formatting | bytes 1572864
